TPU v7x, 256 devices: a whole 4x4x8 slice. The times are simulated.
256 devices in a mesh: ctx: 32 (over y, x, core), head: 8 (over z).
Axes of the slice: x: 4, y: 4, z: 8, core: 2. Of those that a mesh axis runs over, the one named last changes fastest.
Arguments:
- queries: bfloat16 [32768, 4096], P('ctx', 'head'), may hold values from -1.796875 to 1.796875
- keys: bfloat16 [32768, 4096], P('ctx', 'head'), may hold values from -1.796875 to 1.796875
- values: bfloat16 [32768, 4096], P('ctx', 'head'), may hold values from -6 to 6
- gate: bfloat16 [32768, 4096], P('ctx', 'head'), may hold values from -6 to 6
- grad_out: bfloat16 [32768, 4096], P('ctx', 'head'), may hold values from -6 to 6
- gain: float32 [4096], P('head'), may hold values from 0.5 to 1.5
- decay_rate: float32 [32], P('head'), may hold values from 0 to 1, as said below
- segment_ids: int32 [32768], P('ctx'), may hold values from 0 to 15, never falling along the last dimension, each value on 1 to 8192 neighbouring positions
Outputs:
- grad_queries: bfloat16 [32768, 4096], P('ctx', 'head')
- grad_keys: bfloat16 [32768, 4096], P('ctx', 'head')
- grad_values: bfloat16 [32768, 4096], P('ctx', 'head')
- grad_gate: bfloat16 [32768, 4096], P('ctx', 'head')
- grad_gain: float32 [4096], P('head')
Inputs may be any that keep to these rules, and one draw needn't show every extreme that they name: `segment_ids`: rollout ids never fall along the pack; each rollout holds at most 8192 tokens and one holds exactly 8192. `decay_rate`: positive rates.
All inputs are finite; a program needn't handle non-finite values.
Results may differ from a plain program's by a relative error of at most 0.0049.
Values sent between devices are 32-bit elements; how exact they have to be, the bound alone decides.
A program may use at most 128 MiB of HBM per device.

v0:
```python
import jax
import jax.numpy as jnp
from jax import lax
from jax.sharding import PartitionSpec as P

BLOCK = 256


def passed_along(block, axis, distance):
    devices = range(lax.axis_size(axis))
    route = [(i - distance, i) for i in devices if i - distance in devices]
    return lax.ppermute(block, axis, route)


def combine(early, later):
    ehead, etail, eprod, estate = early
    lhead, ltail, lprod, lstate = later
    link = (lhead == ltail) & ((etail == lhead) | (lhead < 0))
    linked = link.astype(jnp.float32)[0]
    state = linked * lprod[:, None, None] * estate + lstate
    head = jnp.where(ehead < 0, lhead, ehead)
    tail = jnp.where(ltail < 0, etail, ltail)
    return (head, tail, eprod * lprod, state)


def body(queries, keys, values, gate, grad_out, gain, decay_rate, segment_ids):
    hi = lax.Precision.HIGHEST
    tok_rows = queries.shape[0]
    width = queries.shape[1]
    heads = decay_rate.shape[0]
    hsize = width // heads
    nblocks = tok_rows // BLOCK
    rank = lax.axis_index("ctx")
    ranks = lax.axis_size("ctx")
    logl = -decay_rate

    def split(x):
        return x.astype(jnp.float32).reshape(nblocks, BLOCK, heads, hsize)

    qf = split(queries)
    kf = split(keys)
    vf = split(values)
    segb = segment_ids.reshape(nblocks, BLOCK)
    pos = jnp.arange(BLOCK).astype(jnp.float32)
    diff = pos[:, None] - pos[None, :]
    causal = diff >= 0
    wbase = jnp.where(
        causal[None], jnp.exp(logl[:, None, None] * jnp.where(causal, diff, 0.0)[None]), 0.0
    )
    same = (segb[:, :, None] == segb[:, None, :]).astype(jnp.float32)
    wmask = wbase[None] * same[:, None]
    scores = jnp.einsum("nthd,nshd->nhts", qf, kf, precision=hi) * wmask
    inner = jnp.einsum("nhts,nshe->nthe", scores, vf, precision=hi)
    firsts = segb[:, 0]
    lasts = segb[:, -1]
    pfull = jnp.exp(logl * BLOCK)
    wlast = (
        jnp.exp(logl[None, None, :] * (BLOCK - 1.0 - pos)[None, :, None])
        * (segb == lasts[:, None]).astype(jnp.float32)[:, :, None]
    )
    fsum = jnp.einsum("nshd,nshe->nhde", kf * wlast[..., None], vf, precision=hi)
    identity = (
        jnp.full((1,), -1, jnp.int32),
        jnp.full((1,), -1, jnp.int32),
        jnp.ones((heads,), jnp.float32),
        jnp.zeros((heads, hsize, hsize), jnp.float32),
    )

    def fwd_elem(n):
        return (firsts[n : n + 1], lasts[n : n + 1], pfull, fsum[n])

    own = identity
    for n in range(nblocks):
        own = combine(own, fwd_elem(n))

    def fwd_turn(i, carry):
        incl, recv = carry
        got = passed_along((incl[0], incl[1], incl[2], incl[3]), "ctx", 1)
        valid = rank > 0
        got = (
            jnp.where(valid, got[0], -1),
            jnp.where(valid, got[1], -1),
            jnp.where(valid, got[2], 1.0),
            got[3],
        )
        return (combine(got, own), got)

    incoming = lax.fori_loop(0, ranks - 1, fwd_turn, (own, identity))[1]
    cur = incoming
    fwd_states = []
    fwd_labels = []
    for n in range(nblocks):
        fwd_states.append(cur[3])
        fwd_labels.append(cur[1])
        cur = combine(cur, fwd_elem(n))
    sin = jnp.stack(fwd_states)
    flabel = jnp.concatenate(fwd_labels)
    coef = (
        jnp.exp(logl[None, None, :] * (pos + 1.0)[None, :, None])
        * (segb == flabel[:, None]).astype(jnp.float32)[:, :, None]
    )
    cross = jnp.einsum("nthd,nhde->nthe", qf, sin, precision=hi) * coef[..., None]
    attn = (inner + cross).reshape(tok_rows, width)
    sig = jax.nn.sigmoid(gate.astype(jnp.float32))
    upper = grad_out.astype(jnp.float32)
    dz = upper * sig * gain
    squares, crossed = lax.psum(
        (jnp.sum(attn * attn, axis=-1), jnp.sum(dz * attn, axis=-1)), "head"
    )
    feats = width * lax.axis_size("head")
    ratio = lax.rsqrt(squares / feats + 1e-06)
    normed = attn * ratio[:, None]
    grad_gate = (upper * normed * gain * sig * (1.0 - sig)).astype(jnp.bfloat16)
    grad_gain = lax.psum(jnp.sum(upper * sig * normed, axis=0), "ctx")
    datt = (ratio[:, None] * dz - (ratio * ratio * ratio * crossed / feats)[:, None] * attn).astype(
        jnp.bfloat16
    )
    df = split(datt)
    wfirst = (
        jnp.exp(logl[None, None, :] * pos[None, :, None])
        * (segb == firsts[:, None]).astype(jnp.float32)[:, :, None]
    )
    rsum = jnp.einsum("nthd,nthe->nhde", qf * wfirst[..., None], df, precision=hi)

    def rev_elem(n):
        return (lasts[n : n + 1], firsts[n : n + 1], pfull, rsum[n])

    own_rev = identity
    for n in reversed(range(nblocks)):
        own_rev = combine(own_rev, rev_elem(n))

    def rev_turn(i, carry):
        incl, recv = carry
        got = passed_along((incl[0], incl[1], incl[2], incl[3]), "ctx", -1)
        valid = rank < ranks - 1
        got = (
            jnp.where(valid, got[0], -1),
            jnp.where(valid, got[1], -1),
            jnp.where(valid, got[2], 1.0),
            got[3],
        )
        return (combine(got, own_rev), got)

    incoming_rev = lax.fori_loop(0, ranks - 1, rev_turn, (own_rev, identity))[1]
    cur = incoming_rev
    rev_states = [None] * nblocks
    rev_labels = [None] * nblocks
    for n in reversed(range(nblocks)):
        rev_states[n] = cur[3]
        rev_labels[n] = cur[1]
        cur = combine(cur, rev_elem(n))
    rin = jnp.stack(rev_states)
    rlabel = jnp.concatenate(rev_labels)
    coefr = (
        jnp.exp(logl[None, None, :] * (BLOCK - pos)[None, :, None])
        * (segb == rlabel[:, None]).astype(jnp.float32)[:, :, None]
    )
    dscore = jnp.einsum("nthe,nshe->nhts", df, vf, precision=hi) * wmask
    grad_q = (
        jnp.einsum("nhts,nshd->nthd", dscore, kf, precision=hi)
        + jnp.einsum("nthe,nhde->nthd", df, sin, precision=hi) * coef[..., None]
    )
    grad_k = (
        jnp.einsum("nhts,nthd->nshd", dscore, qf, precision=hi)
        + jnp.einsum("nshe,nhde->nshd", vf, rin, precision=hi) * coefr[..., None]
    )
    grad_v = (
        jnp.einsum("nhts,nthe->nshe", scores, df, precision=hi)
        + jnp.einsum("nshd,nhde->nshe", kf, rin, precision=hi) * coefr[..., None]
    )
    return (
        grad_q.reshape(tok_rows, width).astype(jnp.bfloat16),
        grad_k.reshape(tok_rows, width).astype(jnp.bfloat16),
        grad_v.reshape(tok_rows, width).astype(jnp.bfloat16),
        grad_gate,
        grad_gain,
    )


def solution(mesh):
    in_specs = (
        P("ctx", "head"),
        P("ctx", "head"),
        P("ctx", "head"),
        P("ctx", "head"),
        P("ctx", "head"),
        P("head"),
        P("head"),
        P("ctx"),
    )
    out_specs = (P("ctx", "head"), P("ctx", "head"), P("ctx", "head"), P("ctx", "head"), P("head"))
    return jax.shard_map(body, mesh=mesh, in_specs=in_specs, out_specs=out_specs, check_vma=False)
```

profile of v0, /device:TPU:1, one launch (start us, length us, event | category | flops | bytes accessed | tf_op | source)
XLA Modules:
  0.0 976.7 jit_solution(1084432816046583037)
XLA Ops:
  39.7 6.7 fusion.1
  53.7 374.8 %while.36 = (s32[]{:T(128)}, s32[1]{0:T(128)}, f32[4,128,128]{2,1,0:T(8,128)}, s32[1]{0:T(128)}, f32[4,128,128]{2,1,0:T(8,128)}, /*index=5*/pred[]{:T(512)}, pre...) while((s32[]{:T(128)}, s32[1]{0:T(128)}, ...), condition=%wide.region_1.2_spmd, body=%wide.region_0.1_spmd.sunk | while | flops 131084 | bytes 2883947 | solution.py:88
  128.0 6.4 collective-permute-start.1
  140.5 6.4 collective-permute-start.1
  153.0 6.4 collective-permute-start.1
  165.6 6.4 collective-permute-start.1
  178.1 6.4 collective-permute-start.1
  190.6 6.4 collective-permute-start.1
  203.1 6.4 collective-permute-start.1
  215.6 6.4 collective-permute-start.1
  240.7 6.4 collective-permute-start.1
  253.2 6.4 collective-permute-start.1
  290.8 6.4 collective-permute-start.1
  303.3 6.4 collective-permute-start.1
  340.9 6.4 collective-permute-start.1
  353.4 6.4 collective-permute-start.1
  378.4 6.4 collective-permute-start.1
  391.0 6.4 collective-permute-start.1
  403.5 6.4 collective-permute-start.1
  441.0 16.2 %psum.21 = f32[1024]{0:T(1024)S(1)} all-reduce(f32[1024]{0:T(1024)S(1)} %bitcast.191), channel_id=1, replica_groups=mesh['ctx'=32,'head'=8] {'head'}, use_global_device_ids=true, to_apply=%region_3.4 | all-reduce | flops 1024 | bytes 8192 | tf_op jit(solution)/shard_map/psum | solution.py:107
  461.7 10.7 %psum.22 = f32[1024]{0:T(1024)S(1)} all-reduce(f32[1024]{0:T(1024)S(1)} %get-tuple-element.266), channel_id=1, replica_groups=mesh['ctx'=32,'head'=8] {'head'}, use_global_device_ids=true, to_apply=%region_5.6 | all-reduce | flops 1024 | bytes 8192 | tf_op jit(solution)/shard_map/psum | solution.py:107
  489.2 385.5 %while.37 = (s32[]{:T(128)}, s32[1]{0:T(128)}, f32[4,128,128]{2,1,0:T(8,128)}, s32[1]{0:T(128)}, f32[4,128,128]{2,1,0:T(8,128)}, /*index=5*/pred[]{:T(512)}, pre...) while((s32[]{:T(128)}, s32[1]{0:T(128)}, ...), condition=%wide.region_7.8_spmd, body=%wide.region_6.7_spmd.sunk | while | flops 131084 | bytes 2883947 | solution.py:144
  489.2 8.7 collective-permute-start.3
  904.2 72.5 %psum.23 = f32[512]{0:T(512)} all-reduce(f32[512]{0:T(512)S(1)} %get-tuple-element.265), channel_id=1, replica_groups=mesh['ctx'=32,'head'=8] {'ctx'}, use_global_device_ids=true, to_apply=%region_9.10 | all-reduce | flops 512 | bytes 4096 | tf_op jit(solution)/shard_map/psum | solution.py:114
  (581 shorter events, 673.1 us)
Async XLA Ops:
  489.2 18.5 %collective-permute-start.3 = (f32[4,128,128]{2,1,0:T(8,128)}, f32[4,128,128]{2,1,0:T(8,128)S(1)}, u32[]{:S(2)}, u32[]{:S(2)}) collective-permute-start(f32[4,128,128]{2,1,0:T(8,128)} %get-tuple-element.574), channel_id=1, source_target_pairs={{8,0},{16,8},{24,16},{32,24},{40,32},{48,40},{56,48},{64,56},{72,6... | collective-permute-start | bytes 786440 | tf_op jit(solution)/shard_map/while/body/eval_jaxpr/ppermute | solution.py:12
  573.3 10.7 %collective-permute-start.3 = (f32[4,128,128]{2,1,0:T(8,128)}, f32[4,128,128]{2,1,0:T(8,128)S(1)}, u32[]{:S(2)}, u32[]{:S(2)}) collective-permute-start(f32[4,128,128]{2,1,0:T(8,128)} %get-tuple-element.574), channel_id=1, source_target_pairs={{8,0},{16,8},{24,16},{32,24},{40,32},{48,40},{56,48},{64,56},{72,6... | collective-permute-start | bytes 786440 | tf_op jit(solution)/shard_map/while/body/eval_jaxpr/ppermute | solution.py:12
  585.8 10.7 %collective-permute-start.3 = (f32[4,128,128]{2,1,0:T(8,128)}, f32[4,128,128]{2,1,0:T(8,128)S(1)}, u32[]{:S(2)}, u32[]{:S(2)}) collective-permute-start(f32[4,128,128]{2,1,0:T(8,128)} %get-tuple-element.574), channel_id=1, source_target_pairs={{8,0},{16,8},{24,16},{32,24},{40,32},{48,40},{56,48},{64,56},{72,6... | collective-permute-start | bytes 786440 | tf_op jit(solution)/shard_map/while/body/eval_jaxpr/ppermute | solution.py:12
  598.4 10.7 %collective-permute-start.3 = (f32[4,128,128]{2,1,0:T(8,128)}, f32[4,128,128]{2,1,0:T(8,128)S(1)}, u32[]{:S(2)}, u32[]{:S(2)}) collective-permute-start(f32[4,128,128]{2,1,0:T(8,128)} %get-tuple-element.574), channel_id=1, source_target_pairs={{8,0},{16,8},{24,16},{32,24},{40,32},{48,40},{56,48},{64,56},{72,6... | collective-permute-start | bytes 786440 | tf_op jit(solution)/shard_map/while/body/eval_jaxpr/ppermute | solution.py:12
  611.0 10.7 %collective-permute-start.3 = (f32[4,128,128]{2,1,0:T(8,128)}, f32[4,128,128]{2,1,0:T(8,128)S(1)}, u32[]{:S(2)}, u32[]{:S(2)}) collective-permute-start(f32[4,128,128]{2,1,0:T(8,128)} %get-tuple-element.574), channel_id=1, source_target_pairs={{8,0},{16,8},{24,16},{32,24},{40,32},{48,40},{56,48},{64,56},{72,6... | collective-permute-start | bytes 786440 | tf_op jit(solution)/shard_map/while/body/eval_jaxpr/ppermute | solution.py:12
  623.5 10.7 %collective-permute-start.3 = (f32[4,128,128]{2,1,0:T(8,128)}, f32[4,128,128]{2,1,0:T(8,128)S(1)}, u32[]{:S(2)}, u32[]{:S(2)}) collective-permute-start(f32[4,128,128]{2,1,0:T(8,128)} %get-tuple-element.574), channel_id=1, source_target_pairs={{8,0},{16,8},{24,16},{32,24},{40,32},{48,40},{56,48},{64,56},{72,6... | collective-permute-start | bytes 786440 | tf_op jit(solution)/shard_map/while/body/eval_jaxpr/ppermute | solution.py:12
  636.1 10.7 %collective-permute-start.3 = (f32[4,128,128]{2,1,0:T(8,128)}, f32[4,128,128]{2,1,0:T(8,128)S(1)}, u32[]{:S(2)}, u32[]{:S(2)}) collective-permute-start(f32[4,128,128]{2,1,0:T(8,128)} %get-tuple-element.574), channel_id=1, source_target_pairs={{8,0},{16,8},{24,16},{32,24},{40,32},{48,40},{56,48},{64,56},{72,6... | collective-permute-start | bytes 786440 | tf_op jit(solution)/shard_map/while/body/eval_jaxpr/ppermute | solution.py:12
  648.6 10.7 %collective-permute-start.3 = (f32[4,128,128]{2,1,0:T(8,128)}, f32[4,128,128]{2,1,0:T(8,128)S(1)}, u32[]{:S(2)}, u32[]{:S(2)}) collective-permute-start(f32[4,128,128]{2,1,0:T(8,128)} %get-tuple-element.574), channel_id=1, source_target_pairs={{8,0},{16,8},{24,16},{32,24},{40,32},{48,40},{56,48},{64,56},{72,6... | collective-permute-start | bytes 786440 | tf_op jit(solution)/shard_map/while/body/eval_jaxpr/ppermute | solution.py:12
  661.2 10.7 %collective-permute-start.3 = (f32[4,128,128]{2,1,0:T(8,128)}, f32[4,128,128]{2,1,0:T(8,128)S(1)}, u32[]{:S(2)}, u32[]{:S(2)}) collective-permute-start(f32[4,128,128]{2,1,0:T(8,128)} %get-tuple-element.574), channel_id=1, source_target_pairs={{8,0},{16,8},{24,16},{32,24},{40,32},{48,40},{56,48},{64,56},{72,6... | collective-permute-start | bytes 786440 | tf_op jit(solution)/shard_map/while/body/eval_jaxpr/ppermute | solution.py:12
  673.8 10.7 %collective-permute-start.3 = (f32[4,128,128]{2,1,0:T(8,128)}, f32[4,128,128]{2,1,0:T(8,128)S(1)}, u32[]{:S(2)}, u32[]{:S(2)}) collective-permute-start(f32[4,128,128]{2,1,0:T(8,128)} %get-tuple-element.574), channel_id=1, source_target_pairs={{8,0},{16,8},{24,16},{32,24},{40,32},{48,40},{56,48},{64,56},{72,6... | collective-permute-start | bytes 786440 | tf_op jit(solution)/shard_map/while/body/eval_jaxpr/ppermute | solution.py:12
  686.3 10.7 %collective-permute-start.3 = (f32[4,128,128]{2,1,0:T(8,128)}, f32[4,128,128]{2,1,0:T(8,128)S(1)}, u32[]{:S(2)}, u32[]{:S(2)}) collective-permute-start(f32[4,128,128]{2,1,0:T(8,128)} %get-tuple-element.574), channel_id=1, source_target_pairs={{8,0},{16,8},{24,16},{32,24},{40,32},{48,40},{56,48},{64,56},{72,6... | collective-permute-start | bytes 786440 | tf_op jit(solution)/shard_map/while/body/eval_jaxpr/ppermute | solution.py:12
  698.9 10.7 %collective-permute-start.3 = (f32[4,128,128]{2,1,0:T(8,128)}, f32[4,128,128]{2,1,0:T(8,128)S(1)}, u32[]{:S(2)}, u32[]{:S(2)}) collective-permute-start(f32[4,128,128]{2,1,0:T(8,128)} %get-tuple-element.574), channel_id=1, source_target_pairs={{8,0},{16,8},{24,16},{32,24},{40,32},{48,40},{56,48},{64,56},{72,6... | collective-permute-start | bytes 786440 | tf_op jit(solution)/shard_map/while/body/eval_jaxpr/ppermute | solution.py:12
  711.4 10.7 %collective-permute-start.3 = (f32[4,128,128]{2,1,0:T(8,128)}, f32[4,128,128]{2,1,0:T(8,128)S(1)}, u32[]{:S(2)}, u32[]{:S(2)}) collective-permute-start(f32[4,128,128]{2,1,0:T(8,128)} %get-tuple-element.574), channel_id=1, source_target_pairs={{8,0},{16,8},{24,16},{32,24},{40,32},{48,40},{56,48},{64,56},{72,6... | collective-permute-start | bytes 786440 | tf_op jit(solution)/shard_map/while/body/eval_jaxpr/ppermute | solution.py:12
  724.0 10.7 %collective-permute-start.3 = (f32[4,128,128]{2,1,0:T(8,128)}, f32[4,128,128]{2,1,0:T(8,128)S(1)}, u32[]{:S(2)}, u32[]{:S(2)}) collective-permute-start(f32[4,128,128]{2,1,0:T(8,128)} %get-tuple-element.574), channel_id=1, source_target_pairs={{8,0},{16,8},{24,16},{32,24},{40,32},{48,40},{56,48},{64,56},{72,6... | collective-permute-start | bytes 786440 | tf_op jit(solution)/shard_map/while/body/eval_jaxpr/ppermute | solution.py:12
  736.6 10.7 %collective-permute-start.3 = (f32[4,128,128]{2,1,0:T(8,128)}, f32[4,128,128]{2,1,0:T(8,128)S(1)}, u32[]{:S(2)}, u32[]{:S(2)}) collective-permute-start(f32[4,128,128]{2,1,0:T(8,128)} %get-tuple-element.574), channel_id=1, source_target_pairs={{8,0},{16,8},{24,16},{32,24},{40,32},{48,40},{56,48},{64,56},{72,6... | collective-permute-start | bytes 786440 | tf_op jit(solution)/shard_map/while/body/eval_jaxpr/ppermute | solution.py:12
  749.1 10.7 %collective-permute-start.3 = (f32[4,128,128]{2,1,0:T(8,128)}, f32[4,128,128]{2,1,0:T(8,128)S(1)}, u32[]{:S(2)}, u32[]{:S(2)}) collective-permute-start(f32[4,128,128]{2,1,0:T(8,128)} %get-tuple-element.574), channel_id=1, source_target_pairs={{8,0},{16,8},{24,16},{32,24},{40,32},{48,40},{56,48},{64,56},{72,6... | collective-permute-start | bytes 786440 | tf_op jit(solution)/shard_map/while/body/eval_jaxpr/ppermute | solution.py:12
  761.7 10.7 %collective-permute-start.3 = (f32[4,128,128]{2,1,0:T(8,128)}, f32[4,128,128]{2,1,0:T(8,128)S(1)}, u32[]{:S(2)}, u32[]{:S(2)}) collective-permute-start(f32[4,128,128]{2,1,0:T(8,128)} %get-tuple-element.574), channel_id=1, source_target_pairs={{8,0},{16,8},{24,16},{32,24},{40,32},{48,40},{56,48},{64,56},{72,6... | collective-permute-start | bytes 786440 | tf_op jit(solution)/shard_map/while/body/eval_jaxpr/ppermute | solution.py:12
  774.3 10.7 %collective-permute-start.3 = (f32[4,128,128]{2,1,0:T(8,128)}, f32[4,128,128]{2,1,0:T(8,128)S(1)}, u32[]{:S(2)}, u32[]{:S(2)}) collective-permute-start(f32[4,128,128]{2,1,0:T(8,128)} %get-tuple-element.574), channel_id=1, source_target_pairs={{8,0},{16,8},{24,16},{32,24},{40,32},{48,40},{56,48},{64,56},{72,6... | collective-permute-start | bytes 786440 | tf_op jit(solution)/shard_map/while/body/eval_jaxpr/ppermute | solution.py:12
  786.8 10.7 %collective-permute-start.3 = (f32[4,128,128]{2,1,0:T(8,128)}, f32[4,128,128]{2,1,0:T(8,128)S(1)}, u32[]{:S(2)}, u32[]{:S(2)}) collective-permute-start(f32[4,128,128]{2,1,0:T(8,128)} %get-tuple-element.574), channel_id=1, source_target_pairs={{8,0},{16,8},{24,16},{32,24},{40,32},{48,40},{56,48},{64,56},{72,6... | collective-permute-start | bytes 786440 | tf_op jit(solution)/shard_map/while/body/eval_jaxpr/ppermute | solution.py:12
  799.4 10.7 %collective-permute-start.3 = (f32[4,128,128]{2,1,0:T(8,128)}, f32[4,128,128]{2,1,0:T(8,128)S(1)}, u32[]{:S(2)}, u32[]{:S(2)}) collective-permute-start(f32[4,128,128]{2,1,0:T(8,128)} %get-tuple-element.574), channel_id=1, source_target_pairs={{8,0},{16,8},{24,16},{32,24},{40,32},{48,40},{56,48},{64,56},{72,6... | collective-permute-start | bytes 786440 | tf_op jit(solution)/shard_map/while/body/eval_jaxpr/ppermute | solution.py:12
  811.9 10.7 %collective-permute-start.3 = (f32[4,128,128]{2,1,0:T(8,128)}, f32[4,128,128]{2,1,0:T(8,128)S(1)}, u32[]{:S(2)}, u32[]{:S(2)}) collective-permute-start(f32[4,128,128]{2,1,0:T(8,128)} %get-tuple-element.574), channel_id=1, source_target_pairs={{8,0},{16,8},{24,16},{32,24},{40,32},{48,40},{56,48},{64,56},{72,6... | collective-permute-start | bytes 786440 | tf_op jit(solution)/shard_map/while/body/eval_jaxpr/ppermute | solution.py:12
  824.5 10.7 %collective-permute-start.3 = (f32[4,128,128]{2,1,0:T(8,128)}, f32[4,128,128]{2,1,0:T(8,128)S(1)}, u32[]{:S(2)}, u32[]{:S(2)}) collective-permute-start(f32[4,128,128]{2,1,0:T(8,128)} %get-tuple-element.574), channel_id=1, source_target_pairs={{8,0},{16,8},{24,16},{32,24},{40,32},{48,40},{56,48},{64,56},{72,6... | collective-permute-start | bytes 786440 | tf_op jit(solution)/shard_map/while/body/eval_jaxpr/ppermute | solution.py:12
  837.1 10.7 %collective-permute-start.3 = (f32[4,128,128]{2,1,0:T(8,128)}, f32[4,128,128]{2,1,0:T(8,128)S(1)}, u32[]{:S(2)}, u32[]{:S(2)}) collective-permute-start(f32[4,128,128]{2,1,0:T(8,128)} %get-tuple-element.574), channel_id=1, source_target_pairs={{8,0},{16,8},{24,16},{32,24},{40,32},{48,40},{56,48},{64,56},{72,6... | collective-permute-start | bytes 786440 | tf_op jit(solution)/shard_map/while/body/eval_jaxpr/ppermute | solution.py:12
  849.6 10.7 %collective-permute-start.3 = (f32[4,128,128]{2,1,0:T(8,128)}, f32[4,128,128]{2,1,0:T(8,128)S(1)}, u32[]{:S(2)}, u32[]{:S(2)}) collective-permute-start(f32[4,128,128]{2,1,0:T(8,128)} %get-tuple-element.574), channel_id=1, source_target_pairs={{8,0},{16,8},{24,16},{32,24},{40,32},{48,40},{56,48},{64,56},{72,6... | collective-permute-start | bytes 786440 | tf_op jit(solution)/shard_map/while/body/eval_jaxpr/ppermute | solution.py:12
  (183 other events, 1335.0 us)
where the time goes:
time: 989 us; the launch traced here: 977 us
  starting transfers between devices  451 us (46%)
  waiting for transfers between devices  152 us (15%)
  other arithmetic  128 us (13%)
  blocking collectives  99.5 us (10%)
  loops' own time  42.3 us (4%)
  between operations  37.8 us (4%)
  matrix products  36.8 us (4%)
  local copies, waits for them, and re-layouts  29.4 us (3%)
    ppermute x124, starting transfers between devices, passed_along(): return lax.ppermute(block, axis, route)  451 us
    ppermute x124, waiting for transfers between devices, passed_along(): return lax.ppermute(block, axis, route)  152 us
    add x64, other arithmetic, combine(): state = linked * lprod[:, None, None] * estate + lstate  115 us
    psum x1, blocking collectives, body(): grad_gain = lax.psum(jnp.sum(upper * sig * normed, axis=0), 'ctx')  72.5 us
    psum x2, blocking collectives, body(): lax.psum((jnp.sum(attn * attn, axis=-1), jnp.sum(dz * attn, axis=-1)), 'h...  26.9 us
    another operation x1, loops' own time, body(): incoming_rev = lax.fori_loop(0, ranks - 1, rev_turn, (own_rev, identity))[1]  21.5 us
    another operation x1, loops' own time, body(): incoming = lax.fori_loop(0, ranks - 1, fwd_turn, (own, identity))[1]  20.7 us
  transfers between devices with their start and end apart: 124, of which 31 were waited for; matrix products, arithmetic and copies ran while one was open for 0% of the time, Pallas kernels for 0%

commit v1 on v0

v1 whole, which is shorter than its diff:
```python
import functools

import jax
import jax.numpy as jnp
from jax import lax
from jax.experimental import pallas as pl
from jax.experimental.pallas import tpu as pltpu
from jax.sharding import PartitionSpec as P

MESH = pl.DeviceIdType.MESH
F32 = jnp.float32
BF16 = jnp.bfloat16
BLOCK = 256
HD = 128
EPS = 1e-06


def nn(a, b):
    return lax.dot_general(a, b, (((1,), (0,)), ((), ())), preferred_element_type=F32)


def nt(a, b):
    return lax.dot_general(a, b, (((1,), (1,)), ((), ())), preferred_element_type=F32)


def tn(a, b):
    return lax.dot_general(a, b, (((0,), (0,)), ((), ())), preferred_element_type=F32)


def drain(ref, count, sem):
    part = ref.at[pl.ds(0, count)]
    pltpu.make_async_copy(part, part, sem).wait()


def kernel(
    dims,
    q_hbm, k_hbm, v_hbm, g_hbm, o_hbm, gain_ref, rate_ref, seg_ref,
    dq_hbm, dk_hbm, dv_hbm, gg_hbm, dgain_ref,
    qv, kv, vv, gv, ov, segc, wl, wf, wb, fst, sw, attn, gs, sst, bc, qwt, datt, rst,
    dkp, dvp, dqv, dkv, dvv, ggv,
    fbuf, rbuf, sbuf, ebuf, fbuf2, rbuf2, sbuf2, ebuf2, lab, flab, rlab, zbuf, gbuf, cbuf,
    in_sem, out_sem, ssem, rsem,
):
    R, Z, RW, N, H = dims
    T = N * BLOCK
    J = R // H
    SR = H * HD // R
    CW = R // RW
    me = lax.axis_index("ctx")
    zme = lax.axis_index("head")
    row0 = (me // RW) * RW
    mcol = me - row0
    mrow = me // RW
    hm = lax.rem(me, H)
    jm = me // H
    myslice = hm * J + jm

    loads = [
        pltpu.make_async_copy(src, dst, in_sem.at[i])
        for i, (src, dst) in enumerate(
            ((k_hbm, kv), (v_hbm, vv), (q_hbm, qv), (g_hbm, gv), (o_hbm, ov))
        )
    ]
    loads[0].start()
    loads[1].start()

    barrier = pltpu.get_barrier_semaphore()

    def greet_ctx(i, c):
        pl.semaphore_signal(
            barrier, inc=1, device_id=(lax.rem(me + i, R), zme), device_id_type=MESH
        )
        return c

    def greet_head(i, c):
        pl.semaphore_signal(
            barrier, inc=1, device_id=(me, lax.rem(zme + i, Z)), device_id_type=MESH
        )
        return c

    lax.fori_loop(1, R, greet_ctx, 0)
    lax.fori_loop(1, Z, greet_head, 0)
    for i in (2, 3, 4):
        loads[i].start()

    def remote(src, dst, phase, ctx, head):
        return pltpu.make_async_remote_copy(
            src_ref=src, dst_ref=dst, send_sem=ssem.at[phase], recv_sem=rsem.at[phase],
            device_id=(ctx, head), device_id_type=MESH,
        )

    def col(h):
        return slice(h * HD, (h + 1) * HD)

    def rows(n):
        start = n * BLOCK
        return pl.ds(start if isinstance(n, int) else pl.multiple_of(start, BLOCK), BLOCK)

    def power(h, times):
        return jnp.exp(jnp.full((1, HD), -rate_ref[h] * times, F32))

    iota = lax.broadcasted_iota(jnp.int32, (BLOCK, HD), 0).astype(F32)
    for h in range(H):
        wl[h] = jnp.exp(-rate_ref[h] * (BLOCK - 1.0 - iota))
    first_row = jnp.where(lax.broadcasted_iota(jnp.int32, (16, HD), 0) == 0, 1.0, 0.0).astype(BF16)
    for n in range(N):
        seg = jnp.broadcast_to(seg_ref[0:1, rows(n)].astype(F32), (16, BLOCK)).astype(BF16)
        segc[rows(n), :] = tn(seg, first_row)
    lab[me] = jnp.concatenate([segc[T - 1 : T, :], segc[0:1, :]], axis=0)
    lam = [power(h, 1.0) for h in range(H)]
    pblock = [power(h, float(BLOCK)) for h in range(H)]

    def scatter_head(h, src, dst, phase):
        def step(i, c):
            j = lax.rem(i + jm, J)
            dest = H * j + h

            @pl.when(dest != me)
            def _():
                remote(src.at[h * J + j], dst.at[me], phase, dest, zme).start()

            return c

        lax.fori_loop(0, J, step, 0)

    loads[0].wait()
    loads[1].wait()
    for h in range(H):
        own = None
        for n in range(N):
            last = segc[n * BLOCK + BLOCK - 1 : n * BLOCK + BLOCK, :]
            here = segc[rows(n), :] == last
            kw = jnp.where(here, kv[rows(n), col(h)].astype(F32) * wl[h], 0.0).astype(BF16)
            f = tn(kw, vv[rows(n), col(h)])
            fst[n, h] = f
            if own is None:
                own = f
            else:
                before = segc[n * BLOCK - 1 : n * BLOCK, :]
                own = jnp.where(before == last, pblock[h], 0.0) * own + f
        fbuf[h * J : (h + 1) * J] = own.reshape(J, SR, HD)
        if h == 0:
            pl.semaphore_wait(barrier, R - 1 + Z - 1)

            def label_row(i, c):
                remote(lab.at[me], lab.at[me], 0, row0 + lax.rem(mcol + i, RW), zme).start()
                return c

            lax.fori_loop(1, RW, label_row, 0)
        scatter_head(h, fbuf, rbuf, 2)
    rbuf[me] = fbuf[myslice]

    drain(lab, RW - 1, rsem.at[0])
    mine = lab.at[pl.ds(row0, RW)]

    def label_col(i, c):
        other = lax.rem(mrow + i, CW)
        remote(mine, mine, 1, other * RW + mcol, zme).start()
        return c

    lax.fori_loop(1, CW, label_col, 0)

    d2 = (
        lax.broadcasted_iota(jnp.int32, (BLOCK, BLOCK), 0)
        - lax.broadcasted_iota(jnp.int32, (BLOCK, BLOCK), 1)
    ).astype(F32)
    for h in range(H):
        wf[h] = jnp.exp(-rate_ref[h] * iota)
        wb[h] = jnp.where(d2 >= 0, jnp.exp(-rate_ref[h] * jnp.maximum(d2, 0.0)), 0.0)

    def same_of(n):
        sc = segc[rows(n), :]
        return jnp.concatenate([sc, sc], axis=1) == seg_ref[0:1, rows(n)].astype(F32)

    def intra(n, c):
        same = same_of(n)
        for h in range(H):
            s = nt(qv[rows(n), col(h)], kv[rows(n), col(h)])
            s = jnp.where(same, s * wb[h], 0.0).astype(BF16)
            sw[n, h] = s
            attn[rows(n), col(h)] = nn(s, vv[rows(n), col(h)])
            sig = jax.nn.sigmoid(gv[rows(n), col(h)].astype(F32))
            gs[rows(n), col(h)] = ov[rows(n), col(h)].astype(F32) * sig
        return c

    for i in (2, 3, 4):
        loads[i].wait()
    lax.fori_loop(0, N // 2, intra, 0)

    def spread(sb, eb, phase):
        def step(i, c):
            dest = lax.rem(me + i, R)
            remote(sb.at[dest], eb.at[myslice], phase, dest, zme).start()
            return c

        lax.fori_loop(1, R, step, 0)
        eb[myslice] = sb[me]

    drain(lab, R - RW, rsem.at[1])
    drain(rbuf, R - 1, rsem.at[2])
    pdev = power(hm, float(T))
    acc = jnp.zeros((SR, HD), F32)
    for r in range(R - 1):
        sbuf[r] = acc
        if r == 0:
            acc = rbuf[r]
        else:
            linked = lab[r - 1, 0:1, :] == lab[r, 0:1, :]
            acc = rbuf[r] + jnp.where(linked, pdev, 0.0) * acc
    sbuf[R - 1] = acc
    spread(sbuf, ebuf, 3)

    lax.fori_loop(N // 2, N, intra, 0)

    flab[0] = lab[jnp.maximum(me - 1, 0), 0:1, :]
    rlab[N - 1] = lab[jnp.minimum(me + 1, R - 1), 1:2, :]
    for n in range(1, N):
        flab[n] = segc[n * BLOCK - 1 : n * BLOCK, :]
        rlab[n - 1] = segc[n * BLOCK : n * BLOCK + 1, :]
    drain(ebuf, R - 1, rsem.at[3])
    for h in range(H):
        state = lam[h] * ebuf[h * J : (h + 1) * J].reshape(HD, HD)
        for n in range(N):
            sst[n, h] = state.astype(BF16)
            if n < N - 1:
                keep = flab[n] == flab[n + 1]
                state = jnp.where(keep, pblock[h], 0.0) * state + lam[h] * fst[n, h]

    row16 = lax.broadcasted_iota(jnp.int32, (16, HD), 0)

    def cross(n, total):
        linked = segc[rows(n), :] == flab[n]
        ssq = jnp.zeros((BLOCK, HD), F32)
        sda = jnp.zeros((BLOCK, HD), F32)
        for h in range(H):
            c = nn(qv[rows(n), col(h)], sst[n, h])
            a = attn[rows(n), col(h)] + jnp.where(linked, wf[h], 0.0) * c
            attn[rows(n), col(h)] = a
            ssq = ssq + a * a
            sda = sda + (gs[rows(n), col(h)] * gain_ref[0:1, col(h)]) * a
        pick1 = jnp.where(row16 == n, 1.0, 0.0).astype(BF16)
        pick2 = jnp.where(row16 == n + N, 1.0, 0.0).astype(BF16)
        return total + nt(pick1, ssq.astype(BF16)) + nt(pick2, sda.astype(BF16))

    total = lax.fori_loop(0, N, cross, jnp.zeros((16, BLOCK), F32))
    zbuf[zme] = total[0 : 2 * N, :]

    def send_head(i, c):
        remote(zbuf.at[zme], zbuf.at[zme], 4, me, lax.rem(zme + i, Z)).start()
        return c

    lax.fori_loop(1, Z, send_head, 0)

    def turn(n, c):
        first = segc[pl.ds(n * BLOCK, 1), :]
        here = segc[rows(n), :] == first
        for h in range(H):
            qw = jnp.where(here, qv[rows(n), col(h)].astype(F32) * wf[h], 0.0)
            qwt[n, h] = qw.T.astype(BF16)
        return c

    lax.fori_loop(0, N, turn, 0)

    drain(zbuf, Z - 1, rsem.at[4])
    tot = zbuf[0]
    for i in range(1, Z):
        tot = tot + zbuf[i]
    feats = float(H * HD * Z)
    rat = lax.rsqrt(tot[0:N] / feats + EPS)
    cor = rat * rat * rat * (tot[N : 2 * N] / feats)
    both = jnp.concatenate([rat, cor], axis=0)
    upper = both.astype(BF16).astype(F32)
    lhs = jnp.concatenate([upper, both - upper], axis=0).astype(BF16)
    wide = 2 * N * HD
    rr = lax.broadcasted_iota(jnp.int32, (4 * N, wide), 0)
    cc = lax.broadcasted_iota(jnp.int32, (4 * N, wide), 1) // HD
    picks = jnp.where((rr == cc) | (rr == cc + 2 * N), 1.0, 0.0).astype(BF16)
    bc[...] = tn(lhs, picks)

    def factor(n):
        if isinstance(n, int):
            return bc[:, n * HD : (n + 1) * HD]
        return bc[:, pl.ds(pl.multiple_of(n * HD, HD), HD)]

    for h in range(H):
        own = None
        for n in reversed(range(N)):
            dz = gs[rows(n), col(h)] * gain_ref[0:1, col(h)]
            d = (factor(n) * dz - factor(N + n) * attn[rows(n), col(h)]).astype(BF16)
            datt[rows(n), col(h)] = d
            f = nn(qwt[n, h], d)
            rst[n, h] = f
            if own is None:
                own = f
            else:
                first = segc[n * BLOCK : n * BLOCK + 1, :]
                after = segc[(n + 1) * BLOCK : (n + 1) * BLOCK + 1, :]
                own = jnp.where(first == after, pblock[h], 0.0) * own + f
        fbuf2[h * J : (h + 1) * J] = own.reshape(J, SR, HD)
        scatter_head(h, fbuf2, rbuf2, 5)
    rbuf2[me] = fbuf2[myslice]

    def gated(n, sums):
        out = []
        for h in range(H):
            normed = attn[rows(n), col(h)] * factor(n)
            t = gs[rows(n), col(h)] * normed
            sig = jax.nn.sigmoid(gv[rows(n), col(h)].astype(F32))
            ggv[rows(n), col(h)] = (t * gain_ref[0:1, col(h)] * (1.0 - sig)).astype(BF16)
            out.append(sums[h] + jnp.sum(t.reshape(BLOCK // 8, 8, HD), axis=0))
        return tuple(out)

    sums = lax.fori_loop(0, N, gated, tuple(jnp.zeros((8, HD), F32) for _ in range(H)))
    gbuf[mcol] = jnp.concatenate([jnp.sum(s, axis=0, keepdims=True) for s in sums], axis=1)
    out_gg = pltpu.make_async_copy(ggv, gg_hbm, out_sem.at[3])
    out_gg.start()

    def gain_row(i, c):
        remote(gbuf.at[mcol], gbuf.at[mcol], 6, row0 + lax.rem(mcol + i, RW), zme).start()
        return c

    lax.fori_loop(1, RW, gain_row, 0)

    def back(n, c):
        same = same_of(n)
        linked = segc[rows(n), :] == flab[n]
        for h in range(H):
            d = datt[rows(n), col(h)]
            s = nt(d, vv[rows(n), col(h)])
            ds = jnp.where(same, s * wb[h], 0.0).astype(BF16)
            dq = nn(ds, kv[rows(n), col(h)])
            dq = dq + jnp.where(linked, wf[h], 0.0) * nt(d, sst[n, h])
            dqv[rows(n), col(h)] = dq.astype(BF16)
            dkp[rows(n), col(h)] = tn(ds, qv[rows(n), col(h)])
            dvp[rows(n), col(h)] = tn(sw[n, h], d)
        return c

    lax.fori_loop(0, N // 2, back, 0)

    drain(rbuf2, R - 1, rsem.at[5])
    acc = jnp.zeros((SR, HD), F32)
    for r in reversed(range(1, R)):
        sbuf2[r] = acc
        if r == R - 1:
            acc = rbuf2[r]
        else:
            linked = lab[r + 1, 1:2, :] == lab[r, 1:2, :]
            acc = rbuf2[r] + jnp.where(linked, pdev, 0.0) * acc
    sbuf2[0] = acc
    spread(sbuf2, ebuf2, 7)

    drain(gbuf, RW - 1, rsem.at[6])
    part = gbuf[0]
    for i in range(1, RW):
        part = part + gbuf[i]
    cbuf[mrow] = part

    def gain_col(i, c):
        other = lax.rem(mrow + i, CW)
        remote(cbuf.at[mrow], cbuf.at[mrow], 8, other * RW + mcol, zme).start()
        return c

    lax.fori_loop(1, CW, gain_col, 0)

    lax.fori_loop(N // 2, N, back, 0)
    out_dq = pltpu.make_async_copy(dqv, dq_hbm, out_sem.at[0])
    out_dq.start()

    drain(ebuf2, R - 1, rsem.at[7])
    states = [lam[h] * ebuf2[h * J : (h + 1) * J].reshape(HD, HD) for h in range(H)]
    outs = []
    for n in reversed(range(N)):
        linked = segc[rows(n), :] == rlab[n]
        for h in range(H):
            rin = states[h].astype(BF16)
            w = jnp.where(linked, wl[h], 0.0)
            dk = dkp[rows(n), col(h)] + w * nt(vv[rows(n), col(h)], rin)
            dv = dvp[rows(n), col(h)] + w * nn(kv[rows(n), col(h)], rin)
            dkv[rows(n), col(h)] = dk.astype(BF16)
            dvv[rows(n), col(h)] = dv.astype(BF16)
            if n > 0:
                keep = rlab[n] == rlab[n - 1]
                states[h] = jnp.where(keep, pblock[h], 0.0) * states[h] + lam[h] * rst[n, h]
        for src, dst, slot in ((dkv, dk_hbm, 4 + n), (dvv, dv_hbm, 4 + N + n)):
            copy = pltpu.make_async_copy(src.at[rows(n)], dst.at[rows(n)], out_sem.at[slot])
            copy.start()
            outs.append(copy)

    drain(cbuf, CW - 1, rsem.at[8])
    part = cbuf[0]
    for i in range(1, CW):
        part = part + cbuf[i]
    dgain_ref[...] = part

    drain(lab, RW - 1, ssem.at[0])
    drain(lab, R - RW, ssem.at[1])
    drain(fbuf, R - 1, ssem.at[2])
    drain(sbuf, R - 1, ssem.at[3])
    drain(zbuf, Z - 1, ssem.at[4])
    drain(fbuf2, R - 1, ssem.at[5])
    drain(gbuf, RW - 1, ssem.at[6])
    drain(sbuf2, R - 1, ssem.at[7])
    drain(cbuf, CW - 1, ssem.at[8])
    out_gg.wait()
    out_dq.wait()
    for copy in outs:
        copy.wait()


def body(queries, keys, values, gate, grad_out, gain, decay_rate, segment_ids):
    R = lax.axis_size("ctx")
    Z = lax.axis_size("head")
    T, W = queries.shape
    H = W // HD
    N = T // BLOCK
    RW = 8 if R == 32 else R // 2
    CW = R // RW
    J = R // H
    SR = H * HD // R
    anyspec = pl.BlockSpec(memory_space=pl.ANY)
    vspec = pl.BlockSpec(memory_space=pltpu.VMEM)
    big = jax.ShapeDtypeStruct((T, W), BF16)
    VM = pltpu.VMEM
    scratch = (
        [VM((T, W), BF16)] * 5
        + [
            VM((T, HD), F32),
            VM((H, BLOCK, HD), F32),
            VM((H, BLOCK, HD), F32),
            VM((H, BLOCK, BLOCK), F32),
            VM((N, H, HD, HD), F32),
            VM((N, H, BLOCK, BLOCK), BF16),
            VM((T, W), F32),
            VM((T, W), F32),
            VM((N, H, HD, HD), BF16),
            VM((BLOCK, 2 * N * HD), F32),
            VM((N, H, HD, BLOCK), BF16),
            VM((T, W), BF16),
            VM((N, H, HD, HD), F32),
            VM((T, W), F32),
            VM((T, W), F32),
        ]
        + [VM((T, W), BF16)] * 4
        + [VM((R, SR, HD), F32)] * 8
        + [
            VM((R, 2, HD), F32),
            VM((N, 1, HD), F32),
            VM((N, 1, HD), F32),
            VM((Z, 2 * N, BLOCK), F32),
            VM((RW, 1, W), F32),
            VM((CW, 1, W), F32),
            pltpu.SemaphoreType.DMA((5,)),
            pltpu.SemaphoreType.DMA((4 + 2 * N,)),
            pltpu.SemaphoreType.DMA((9,)),
            pltpu.SemaphoreType.DMA((9,)),
        ]
    )
    outs = pl.pallas_call(
        functools.partial(kernel, (R, Z, RW, N, H)),
        out_shape=(big, big, big, big, jax.ShapeDtypeStruct((1, W), F32)),
        in_specs=[anyspec] * 5 + [vspec, pl.BlockSpec(memory_space=pltpu.SMEM), vspec],
        out_specs=(anyspec,) * 4 + (vspec,),
        scratch_shapes=scratch,
        compiler_params=pltpu.CompilerParams(
            collective_id=0, has_side_effects=True, vmem_limit_bytes=52 * 1024 * 1024
        ),
    )(
        queries, keys, values, gate, grad_out,
        gain.reshape(1, W), decay_rate, segment_ids.reshape(1, T),
    )
    dq, dk, dv, gg, dgain = outs
    return dq, dk, dv, gg, dgain.reshape(W)


def solution(mesh):
    in_specs = (P("ctx", "head"),) * 5 + (P("head"), P("head"), P("ctx"))
    out_specs = (P("ctx", "head"),) * 4 + (P("head"),)
    return jax.shard_map(body, mesh=mesh, in_specs=in_specs, out_specs=out_specs, check_vma=False)
```

time: 989 us -> 54.1 us (0.05); the launches traced: 977 us -> 53.8 us
  starting transfers between devices: 451 us -> 0 us
  waiting for transfers between devices: 152 us -> 0 us
  other arithmetic: 128 us -> 0 us
  blocking collectives: 99.5 us -> 0 us
  Pallas kernels: 0 us -> 45.4 us
  loops' own time: 42.3 us -> 0 us
  between operations: 37.8 us -> 0.67 us
  matrix products: 36.8 us -> 0 us
  local copies, waits for them, and re-layouts: 29.4 us -> 7.7 us
    ppermute x124 -> x0, starting transfers between devices: 451 us -> none  [passed_along(): return lax.ppermute(block, axis, route)]
    ppermute x124 -> x0, waiting for transfers between devices: 152 us -> none  [passed_along(): return lax.ppermute(block, axis, route)]
    add x65 -> x0, other arithmetic: 115 us -> none  [the longest x64 115 us: combine(): state = linked * lprod[:, None, None] * estate + lstate]
    psum x3 -> x0, blocking collectives: 99.5 us -> none  [the longest x1 72.5 us: body(): grad_gain = lax.psum(jnp.sum(upper * sig * normed, axis=0), 'ctx')]
    pallas_call x0 -> x1, Pallas kernels: none -> 45.4 us  [body(): pl.pallas_call(functools.partial(kernel, (R, Z, RW, N, H)), out_shape=(bi...]
    another operation x2 -> x0, loops' own time: 42.3 us -> none  [the longest x1 21.5 us: body(): incoming_rev = lax.fori_loop(0, ranks - 1, rev_turn, (own_rev, identity))[1]]
    dot_general x12 -> x0, matrix products: 36.8 us -> none  [the longest x1 6.73 us: body(): inner = jnp.einsum('nhts,nshe->nthe', scores, vf, precision=hi)]
    reshape x7 -> x0, local copies, waits for them, and re-layouts: 13.6 us -> none  [split(): return x.astype(jnp.float32).reshape(nblocks, BLOCK, heads, hsize)]
  transfers between devices with their start and end apart: 124 -> 0, of which waited for: 31 -> 0; matrix products, arithmetic and copies ran while one was open for 0% -> 0% of each run, Pallas kernels for 0% -> 0%
where the time goes in v1:
time: 54.1 us; the launch traced here: 53.8 us
  Pallas kernels  45.4 us (84%)
  local copies, waits for them, and re-layouts  7.7 us (14%)
  between operations  0.67 us (1%)
    pallas_call x1, Pallas kernels, body(): pl.pallas_call(functools.partial(kernel, (R, Z, RW, N, H)), out_shape=(bi...  45.4 us
    unnamed x17, local copies, waits for them, and re-layouts  7.7 us

profile of v1, /device:TPU:1, one launch (start us, length us, event | category | flops | bytes accessed | tf_op | source)
XLA Modules:
  0.0 53.8 jit_solution(7642049191681683605)
XLA Ops:
  0.6 0.0 copy-start.1
  0.6 0.0 copy-start.2
  0.7 0.7 %copy-done.1 = f32[512]{0:T(512)S(1)} copy-done((f32[512]{0:T(512)S(1)}, f32[512]{0:T(512)}, u32[]{:S(2)}) %copy-start.1) | copy-done | bytes 2072
  1.3 0.0 copy-done.2
  1.3 0.0 copy-start
  1.3 0.7 %copy-done = s32[1024]{0:T(1024)S(1)} copy-done((s32[1024]{0:T(1024)S(1)}, s32[1024]{0:T(1024)}, u32[]{:S(2)}) %copy-start) | copy-done | bytes 4120
  2.0 45.4 %shard_map.119 = (bf16[1024,512]{1,0:T(8,128)(2,1)S(1)}, bf16[1024,512]{1,0:T(8,128)(2,1)}, bf16[1024,512]{1,0:T(8,128)(2,1)}, bf16[1024,512]{1,0:T(8,128)(2,1)}, f32[1,512]{1,0:T(1,128)S(1)}) custom-call(bf16[1024,512]{1,0:T(8,128)(2,1)} %q_hbm.1, bf16[1024,512]{1,0:T(8,128)(2,1)} %k_hbm.1, bf16[1024,512]{1,0:T(8,128)(2,1)} %v_hbm.1, ...), custom_call_target="tpu_custom_call" | custom-call | tf_op jit(solution)/shard_map/pallas_call | solution.py:458
  47.4 0.0 copy-start.5
  47.4 1.0 %copy.18 = bf16[1024,512]{1,0:T(8,128)(2,1)} copy(bf16[1024,512]{1,0:T(8,128)(2,1)S(1)} %get-tuple-element.20) | data formatting | bytes 2097152
  48.4 0.6 %copy-done.5 = bf16[1024,512]{1,0:T(8,128)(2,1)S(1)} copy-done((bf16[1024,512]{1,0:T(8,128)(2,1)S(1)}, bf16[1024,512]{1,0:T(8,128)(2,1)}, u32[]{:S(2)}) %copy-start.5) | copy-done | bytes 1048600
  49.0 0.0 copy-start.4
  49.0 1.0 %copy.19 = bf16[1024,512]{1,0:T(8,128)(2,1)} copy(bf16[1024,512]{1,0:T(8,128)(2,1)S(1)} %copy-done.5) | data formatting | bytes 2097152
  50.0 0.6 %copy-done.4 = bf16[1024,512]{1,0:T(8,128)(2,1)S(1)} copy-done((bf16[1024,512]{1,0:T(8,128)(2,1)S(1)}, bf16[1024,512]{1,0:T(8,128)(2,1)}, u32[]{:S(2)}) %copy-start.4) | copy-done | bytes 1048600
  50.6 0.0 copy-start.3
  50.6 1.0 %copy.20 = bf16[1024,512]{1,0:T(8,128)(2,1)} copy(bf16[1024,512]{1,0:T(8,128)(2,1)S(1)} %copy-done.4) | data formatting | bytes 2097152
  51.6 0.6 %copy-done.3 = bf16[1024,512]{1,0:T(8,128)(2,1)S(1)} copy-done((bf16[1024,512]{1,0:T(8,128)(2,1)S(1)}, bf16[1024,512]{1,0:T(8,128)(2,1)}, u32[]{:S(2)}) %copy-start.3) | copy-done | bytes 1048600
  52.2 1.0 %copy.21 = bf16[1024,512]{1,0:T(8,128)(2,1)} copy(bf16[1024,512]{1,0:T(8,128)(2,1)S(1)} %copy-done.3) | data formatting | bytes 2097152
  53.2 0.6 %copy.22 = f32[512]{0:T(512)} copy(f32[512]{0:T(512)S(1)} %bitcast.5) | data formatting | bytes 4096
Async XLA Ops:
  0.6 0.7 %copy-start.1 = (f32[512]{0:T(512)S(1)}, f32[512]{0:T(512)}, u32[]{:S(2)}) copy-start(f32[512]{0:T(512)} %param.13) | copy-start | bytes 6148
  0.6 0.7 %copy-start.2 = (f32[4]{0:T(128)S(1)}, f32[4]{0:T(128)}, u32[]{:S(2)}) copy-start(f32[4]{0:T(128)} %rate_ref.1) | copy-start | bytes 52
  1.3 0.7 %copy-start = (s32[1024]{0:T(1024)S(1)}, s32[1024]{0:T(1024)}, u32[]{:S(2)}) copy-start(s32[1024]{0:T(1024)} %param.15) | copy-start | bytes 12292
  47.4 1.6 %copy-start.5 = (bf16[1024,512]{1,0:T(8,128)(2,1)S(1)}, bf16[1024,512]{1,0:T(8,128)(2,1)}, u32[]{:S(2)}) copy-start(bf16[1024,512]{1,0:T(8,128)(2,1)} %get-tuple-element.21) | copy-start | bytes 3145732
  49.0 1.6 %copy-start.4 = (bf16[1024,512]{1,0:T(8,128)(2,1)S(1)}, bf16[1024,512]{1,0:T(8,128)(2,1)}, u32[]{:S(2)}) copy-start(bf16[1024,512]{1,0:T(8,128)(2,1)} %get-tuple-element.22) | copy-start | bytes 3145732
  50.6 1.6 %copy-start.3 = (bf16[1024,512]{1,0:T(8,128)(2,1)S(1)}, bf16[1024,512]{1,0:T(8,128)(2,1)}, u32[]{:S(2)}) copy-start(bf16[1024,512]{1,0:T(8,128)(2,1)} %get-tuple-element.23) | copy-start | bytes 3145732

commit v2 on v1

v2 whole, which is shorter than its diff:
```python
import functools

import jax
import jax.numpy as jnp
from jax import lax
from jax.experimental import pallas as pl
from jax.experimental.pallas import tpu as pltpu
from jax.sharding import PartitionSpec as P

MESH = pl.DeviceIdType.MESH
F32 = jnp.float32
BF16 = jnp.bfloat16
BLOCK = 256
HD = 128
EPS = 1e-06
VMEM_A = 56 * 1024 * 1024


def nn(a, b):
    return lax.dot_general(a, b, (((1,), (0,)), ((), ())), preferred_element_type=F32)


def nt(a, b):
    return lax.dot_general(a, b, (((1,), (1,)), ((), ())), preferred_element_type=F32)


def tn(a, b):
    return lax.dot_general(a, b, (((0,), (0,)), ((), ())), preferred_element_type=F32)


def drain(ref, count, sem):
    part = ref.at[pl.ds(0, count)]
    pltpu.make_async_copy(part, part, sem).wait()


def kernel(
    dims,
    q_hbm, k_hbm, v_hbm, g_hbm, o_hbm, gain_hbm, rate_hbm, seg_hbm,
    dq_hbm, dk_hbm, dv_hbm, gg_hbm, dgain_hbm,
    dqv, dkv, dvv, ggv, dgain_ref, qv, kv, vv, gv, ov, gain_ref, rate_ref, seg_ref,
    segc, wl, wf, wb, fst, sw, attn, gs, sst, bc, qwt, datt, rst, dkp, dvp, ssq, sda,
    pbs0, pbr0, hfs, fen, fbuf0, rbuf0, sbuf0, ebuf0, qbs0, qbr0,
    pbs1, pbr1, fen1, fbuf1, rbuf1, sbuf1, ebuf1, qbs1, qbr1,
    flab, rlab, zbuf, gbuf, cbuf,
    in_sem, out_sem, ssem, rsem,
):
    R, Z, RW, N, H = dims
    T = N * BLOCK
    C = R // 2
    HH = H // 2
    HR = HH * HD
    SR = HR // C
    HJ = C // HH
    CW = R // RW
    CX = 4
    CY = C // CX
    me = lax.axis_index("ctx")
    zme = lax.axis_index("head")
    row0 = (me // RW) * RW
    mcol = me - row0
    mrow = me // RW
    core = lax.rem(me, 2)
    mate = me + 1 - 2 * core
    chip = me // 2
    chipy = chip // CX
    chipx = lax.rem(chip, CX)
    own0 = HH * core
    other0 = HH * (1 - core)

    loads = [
        pltpu.make_async_copy(src, dst, in_sem.at[i])
        for i, (src, dst) in enumerate(
            (
                (seg_hbm, seg_ref), (rate_hbm, rate_ref), (k_hbm, kv), (v_hbm, vv),
                (q_hbm, qv), (g_hbm, gv), (o_hbm, ov), (gain_hbm, gain_ref),
            )
        )
    ]
    for copy in loads[:4]:
        copy.start()

    barrier = pltpu.get_barrier_semaphore()

    def greet(ctx, head):
        pl.semaphore_signal(barrier, inc=1, device_id=(ctx, head), device_id_type=MESH)

    def greet_ctx(i, c):
        greet(lax.rem(me + i, R), zme)
        return c

    def greet_head(i, c):
        greet(me, lax.rem(zme + i, Z))
        return c

    lax.fori_loop(1, Z, greet_head, 0)
    lax.fori_loop(1, R, greet_ctx, 0)
    for copy in loads[4:]:
        copy.start()

    def remote(src, dst, phase, ctx, head):
        return pltpu.make_async_remote_copy(
            src_ref=src, dst_ref=dst, send_sem=ssem.at[phase], recv_sem=rsem.at[phase],
            device_id=(ctx, head), device_id_type=MESH,
        )

    def col(h):
        start = h * HD
        return pl.ds(start if isinstance(h, int) else pl.multiple_of(start, HD), HD)

    def rows(n):
        start = n * BLOCK
        return pl.ds(start if isinstance(n, int) else pl.multiple_of(start, BLOCK), BLOCK)

    def power(h, times):
        return jnp.exp(jnp.full((1, HD), -rate_ref[h] * times, F32))

    iota = lax.broadcasted_iota(jnp.int32, (BLOCK, HD), 0).astype(F32)
    first_row = jnp.where(lax.broadcasted_iota(jnp.int32, (16, HD), 0) == 0, 1.0, 0.0).astype(BF16)
    loads[0].wait()
    for n in range(N):
        seg = jnp.broadcast_to(seg_ref[0:1, rows(n)].astype(F32), (16, BLOCK)).astype(BF16)
        segc[rows(n), :] = tn(seg, first_row)
    loads[1].wait()
    for h in range(H):
        wl[h] = jnp.exp(-rate_ref[h] * (BLOCK - 1.0 - iota))
    mylast = segc[T - 1 : T, :]
    myfirst = segc[0:1, :]

    def reach(o):
        return min(o[0], CY - o[0]) + min(o[1], CX - o[1])

    offsets = sorted(
        ((dy, dx) for dy in range(CY) for dx in range(CX) if dy or dx), key=reach, reverse=True
    )

    def each_chip(send):
        for dy, dx in offsets:
            send(lax.rem(chipy + dy, CY) * CX + lax.rem(chipx + dx, CX))

    def merge(entry, pbr, lab_m, lab_p, fen_ref, fbuf):
        is_entry = core == entry
        lab_entry = lax.select(is_entry, lab_m, lab_p)
        lab_exit = lax.select(is_entry, lab_p, lab_m)
        for i in range(HH):
            part = slice(i * HD, (i + 1) * HD)
            fm = hfs[part, :]
            fp = pbr[part, :]
            fe = lax.select(is_entry, fm, fp)
            fx = lax.select(is_entry, fp, fm)
            fen_ref[part, :] = fe
            c = fx + jnp.where(lab_entry == lab_exit, power(own0 + i, float(T)), 0.0) * fe
            fbuf[i * HJ : (i + 1) * HJ, 0:SR, :] = c.reshape(HJ, SR, HD)
        return lab_entry, lab_exit

    def hand_over(entry, fen_ref, ebuf, lab_entry, lab_in, qbs):
        is_entry = core == entry
        kept = []
        for i in range(HH):
            part = slice(i * HD, (i + 1) * HD)
            ve = ebuf[i * HJ : (i + 1) * HJ].reshape(HD, HD)
            linked = jnp.where(lab_in == lab_entry, power(own0 + i, float(T)), 0.0)
            vx = fen_ref[part, :] + linked * ve
            qbs[part, :] = lax.select(is_entry, vx, ve)
            kept.append(lax.select(is_entry, ve, vx))
        return kept, lax.select(is_entry, lab_in, lab_entry)

    def device_state(h):
        own = None
        pb = power(h, float(BLOCK))
        w = wl[h]
        for n in range(N):
            last = segc[n * BLOCK + BLOCK - 1 : n * BLOCK + BLOCK, :]
            here = segc[rows(n), :] == last
            kw = jnp.where(here, kv[rows(n), col(h)].astype(F32) * w, 0.0).astype(BF16)
            f = tn(kw, vv[rows(n), col(h)])
            fst[n, h] = f
            if own is None:
                own = f
            else:
                before = segc[n * BLOCK - 1 : n * BLOCK, :]
                own = jnp.where(before == last, pb, 0.0) * own + f
        return own

    loads[2].wait()
    loads[3].wait()
    for i in range(HH):
        pbs0[i * HD : (i + 1) * HD, :] = device_state(other0 + i)
    top = lax.broadcasted_iota(jnp.int32, (8, HD), 0) == 0
    pbs0[HR : HR + 8, :] = jnp.where(top, mylast, myfirst)
    pl.semaphore_wait(barrier, R - 1 + Z - 1)
    pair0 = remote(pbs0, pbr0, 0, mate, zme)
    pair0.start()
    for i in range(HH):
        hfs[i * HD : (i + 1) * HD, :] = device_state(own0 + i)
    pair0.wait_recv()
    matelast = pbr0[HR : HR + 1, :]
    matefirst = pbr0[HR + 1 : HR + 2, :]
    lab_entry0, lab_exit0 = merge(0, pbr0, mylast, matelast, fen, fbuf0)
    chipfirst = lax.select(core == 0, myfirst, matefirst)
    for c in range(C):
        fbuf0[c, SR : SR + 2, :] = jnp.concatenate([lab_exit0, chipfirst], axis=0)

    def scatter(fbuf, rbuf, phase):
        def send(c):
            remote(fbuf.at[c], rbuf.at[chip], phase, 2 * c + core, zme).start()

        each_chip(send)
        rbuf[chip] = fbuf[chip]

    def spread(sbuf, ebuf, phase):
        def send(c):
            remote(sbuf.at[c], ebuf.at[chip], phase, 2 * c + core, zme).start()

        each_chip(send)
        ebuf[chip] = sbuf[chip]

    scatter(fbuf0, rbuf0, 1)

    d2 = (
        lax.broadcasted_iota(jnp.int32, (BLOCK, BLOCK), 0)
        - lax.broadcasted_iota(jnp.int32, (BLOCK, BLOCK), 1)
    ).astype(F32)
    for h in range(H):
        wf[h] = jnp.exp(-rate_ref[h] * iota)
        wb[h] = jnp.where(d2 >= 0, jnp.exp(-rate_ref[h] * jnp.maximum(d2, 0.0)), 0.0)

    def same_of(n):
        sc = segc[rows(n), :]
        return jnp.concatenate([sc, sc], axis=1) == seg_ref[0:1, rows(n)].astype(F32)

    def intra(n, c):
        same = same_of(n)
        for h in range(H):
            s = nt(qv[rows(n), col(h)], kv[rows(n), col(h)])
            s = jnp.where(same, s * wb[h], 0.0).astype(BF16)
            sw[n, h] = s
            attn[rows(n), col(h)] = nn(s, vv[rows(n), col(h)])
            sig = jax.nn.sigmoid(gv[rows(n), col(h)].astype(F32))
            gs[rows(n), col(h)] = ov[rows(n), col(h)].astype(F32) * sig
        return c

    for copy in loads[4:]:
        copy.wait()
    lax.fori_loop(0, N // 2, intra, 0)

    hold = own0 + chip // HJ
    pchip = power(hold, 2.0 * T)
    drain(rbuf0, C - 1, rsem.at[1])
    acc = jnp.zeros((SR, HD), F32)
    for c in range(C - 1):
        sbuf0[c] = acc
        if c == 0:
            acc = rbuf0[c, 0:SR, :]
        else:
            linked = rbuf0[c - 1, SR : SR + 1, :] == rbuf0[c, SR : SR + 1, :]
            acc = rbuf0[c, 0:SR, :] + jnp.where(linked, pchip, 0.0) * acc
    sbuf0[C - 1] = acc
    spread(sbuf0, ebuf0, 2)

    lax.fori_loop(N // 2, N, intra, 0)

    def chain(h, incoming):
        lam = power(h, 1.0)
        pb = power(h, float(BLOCK))
        state = lam * incoming
        for n in range(N):
            sst[n, h] = state.astype(BF16)
            if n < N - 1:
                keep = flab[n] == flab[n + 1]
                state = jnp.where(keep, pb, 0.0) * state + lam * fst[n, h]

    row16 = lax.broadcasted_iota(jnp.int32, (16, HD), 0)

    def cross(n, h0):
        linked = segc[rows(n), :] == flab[n]
        sq = jnp.zeros((BLOCK, HD), F32)
        da = jnp.zeros((BLOCK, HD), F32)
        for i in range(HH):
            h = h0 + i
            c = nn(qv[rows(n), col(h)], sst[n, h])
            a = attn[rows(n), col(h)] + jnp.where(linked, wf[h], 0.0) * c
            attn[rows(n), col(h)] = a
            sq = sq + a * a
            da = da + (gs[rows(n), col(h)] * gain_ref[0:1, col(h)]) * a
        return sq, da

    def cross_own(n, c):
        sq, da = cross(n, own0)
        ssq[rows(n), :] = sq
        sda[rows(n), :] = da
        return c

    def cross_other(n, total):
        sq, da = cross(n, other0)
        pick1 = jnp.where(row16 == n, 1.0, 0.0).astype(BF16)
        pick2 = jnp.where(row16 == n + N, 1.0, 0.0).astype(BF16)
        sq = (sq + ssq[rows(n), :]).astype(BF16)
        da = (da + sda[rows(n), :]).astype(BF16)
        return total + nt(pick1, sq) + nt(pick2, da)

    lab_in0 = rbuf0[jnp.maximum(chip - 1, 0), SR : SR + 1, :]
    for n in range(1, N):
        flab[n] = segc[n * BLOCK - 1 : n * BLOCK, :]
        rlab[n - 1] = segc[n * BLOCK : n * BLOCK + 1, :]
    drain(ebuf0, C - 1, rsem.at[2])
    kept, label = hand_over(0, fen, ebuf0, lab_entry0, lab_in0, qbs0)
    flab[0] = label
    post0 = remote(qbs0, qbr0, 3, mate, zme)
    post0.start()
    for i in range(HH):
        chain(own0 + i, kept[i])
    lax.fori_loop(0, N, cross_own, 0)
    post0.wait_recv()
    for i in range(HH):
        chain(other0 + i, qbr0[i * HD : (i + 1) * HD, :])
    total = lax.fori_loop(0, N, cross_other, jnp.zeros((16, BLOCK), F32))
    zbuf[zme] = total[0 : 2 * N, :]

    zorder = sorted(range(1, Z), key=lambda i: min(i, Z - i), reverse=True)
    for i in zorder:
        remote(zbuf.at[zme], zbuf.at[zme], 4, me, lax.rem(zme + i, Z)).start()

    def turn(n, c):
        first = segc[pl.ds(n * BLOCK, 1), :]
        here = segc[rows(n), :] == first
        for h in range(H):
            qw = jnp.where(here, qv[rows(n), col(h)].astype(F32) * wf[h], 0.0)
            qwt[n, h] = qw.T.astype(BF16)
        return c

    lax.fori_loop(0, N, turn, 0)

    feats = float(H * HD * Z)
    wide = 2 * N * HD
    rr = lax.broadcasted_iota(jnp.int32, (4 * N, wide), 0)
    cc = lax.broadcasted_iota(jnp.int32, (4 * N, wide), 1) // HD
    picks = jnp.where((rr == cc) | (rr == cc + 2 * N), 1.0, 0.0).astype(BF16)
    drain(zbuf, Z - 1, rsem.at[4])
    tot = zbuf[0]
    for i in range(1, Z):
        tot = tot + zbuf[i]
    rat = lax.rsqrt(tot[0:N] / feats + EPS)
    cor = rat * rat * rat * (tot[N : 2 * N] / feats)
    both = jnp.concatenate([rat, cor], axis=0)
    upper = both.astype(BF16).astype(F32)
    lhs = jnp.concatenate([upper, both - upper], axis=0).astype(BF16)
    bc[...] = tn(lhs, picks)

    def factor(n):
        if isinstance(n, int):
            return bc[:, n * HD : (n + 1) * HD]
        return bc[:, pl.ds(pl.multiple_of(n * HD, HD), HD)]

    def reverse_state(h):
        own = None
        pb = power(h, float(BLOCK))
        for n in reversed(range(N)):
            dz = gs[rows(n), col(h)] * gain_ref[0:1, col(h)]
            d = (factor(n) * dz - factor(N + n) * attn[rows(n), col(h)]).astype(BF16)
            datt[rows(n), col(h)] = d
            f = nn(qwt[n, h], d)
            rst[n, h] = f
            if own is None:
                own = f
            else:
                first = segc[n * BLOCK : n * BLOCK + 1, :]
                after = segc[(n + 1) * BLOCK : (n + 1) * BLOCK + 1, :]
                own = jnp.where(first == after, pb, 0.0) * own + f
        return own

    for i in range(HH):
        pbs1[i * HD : (i + 1) * HD, :] = reverse_state(other0 + i)
    pair1 = remote(pbs1, pbr1, 5, mate, zme)
    pair1.start()
    for i in range(HH):
        hfs[i * HD : (i + 1) * HD, :] = reverse_state(own0 + i)
    pair1.wait_recv()
    lab_entry1, _ = merge(1, pbr1, myfirst, matefirst, fen1, fbuf1)
    scatter(fbuf1, rbuf1, 6)

    def gated(n, sums):
        out = []
        for h in range(H):
            normed = attn[rows(n), col(h)] * factor(n)
            t = gs[rows(n), col(h)] * normed
            sig = jax.nn.sigmoid(gv[rows(n), col(h)].astype(F32))
            ggv[rows(n), col(h)] = (t * gain_ref[0:1, col(h)] * (1.0 - sig)).astype(BF16)
            out.append(sums[h] + jnp.sum(t.reshape(BLOCK // 8, 8, HD), axis=0))
        return tuple(out)

    sums = lax.fori_loop(0, N, gated, tuple(jnp.zeros((8, HD), F32) for _ in range(H)))
    gbuf[mcol] = jnp.concatenate([jnp.sum(s, axis=0, keepdims=True) for s in sums], axis=1)

    def gain_row(i, c):
        remote(gbuf.at[mcol], gbuf.at[mcol], 7, row0 + lax.rem(mcol + i, RW), zme).start()
        return c

    lax.fori_loop(1, RW, gain_row, 0)
    out_gg = pltpu.make_async_copy(ggv, gg_hbm, out_sem.at[0])
    out_gg.start()

    def back(n, c):
        same = same_of(n)
        linked = segc[rows(n), :] == flab[n]
        for h in range(H):
            d = datt[rows(n), col(h)]
            s = nt(d, vv[rows(n), col(h)])
            ds = jnp.where(same, s * wb[h], 0.0).astype(BF16)
            dq = nn(ds, kv[rows(n), col(h)])
            dq = dq + jnp.where(linked, wf[h], 0.0) * nt(d, sst[n, h])
            dqv[rows(n), col(h)] = dq.astype(BF16)
            dkp[rows(n), col(h)] = tn(ds, qv[rows(n), col(h)])
            dvp[rows(n), col(h)] = tn(sw[n, h], d)
        return c

    lax.fori_loop(0, N // 2, back, 0)

    drain(rbuf1, C - 1, rsem.at[6])
    acc = jnp.zeros((SR, HD), F32)
    for c in reversed(range(1, C)):
        sbuf1[c] = acc
        if c == C - 1:
            acc = rbuf1[c]
        else:
            linked = rbuf0[c + 1, SR + 1 : SR + 2, :] == rbuf0[c, SR + 1 : SR + 2, :]
            acc = rbuf1[c] + jnp.where(linked, pchip, 0.0) * acc
    sbuf1[0] = acc
    spread(sbuf1, ebuf1, 8)

    drain(gbuf, RW - 1, rsem.at[7])
    part = gbuf[0]
    for i in range(1, RW):
        part = part + gbuf[i]
    cbuf[mrow] = part

    def gain_col(i, c):
        other = lax.rem(mrow + i, CW)
        remote(cbuf.at[mrow], cbuf.at[mrow], 9, other * RW + mcol, zme).start()
        return c

    lax.fori_loop(1, CW, gain_col, 0)

    lax.fori_loop(N // 2, N, back, 0)
    out_dq = pltpu.make_async_copy(dqv, dq_hbm, out_sem.at[1])
    out_dq.start()

    drain(cbuf, CW - 1, rsem.at[9])
    part = cbuf[0]
    for i in range(1, CW):
        part = part + cbuf[i]
    dgain_ref[...] = part
    out_gain = pltpu.make_async_copy(dgain_ref, dgain_hbm, out_sem.at[2])
    out_gain.start()

    def finish(h, incoming):
        lam = power(h, 1.0)
        pb = power(h, float(BLOCK))
        state = lam * incoming
        for n in reversed(range(N)):
            rin = state.astype(BF16)
            w = jnp.where(segc[rows(n), :] == rlab[n], wl[h], 0.0)
            dk = dkp[rows(n), col(h)] + w * nt(vv[rows(n), col(h)], rin)
            dv = dvp[rows(n), col(h)] + w * nn(kv[rows(n), col(h)], rin)
            dkv[rows(n), col(h)] = dk.astype(BF16)
            dvv[rows(n), col(h)] = dv.astype(BF16)
            if n > 0:
                keep = rlab[n] == rlab[n - 1]
                state = jnp.where(keep, pb, 0.0) * state + lam * rst[n, h]

    lab_in1 = rbuf0[jnp.minimum(chip + 1, C - 1), SR + 1 : SR + 2, :]
    drain(ebuf1, C - 1, rsem.at[8])
    kept, label = hand_over(1, fen1, ebuf1, lab_entry1, lab_in1, qbs1)
    rlab[N - 1] = label
    post1 = remote(qbs1, qbr1, 10, mate, zme)
    post1.start()
    outs = [out_gg, out_dq, out_gain]

    def put(h0, slot):
        part = pl.ds(pl.multiple_of(h0 * HD, HD), HH * HD)
        for i, (src, dst) in enumerate(((dkv, dk_hbm), (dvv, dv_hbm))):
            copy = pltpu.make_async_copy(src.at[:, part], dst.at[:, part], out_sem.at[slot + i])
            copy.start()
            outs.append(copy)

    for i in range(HH):
        finish(own0 + i, kept[i])
    put(own0, 3)
    post1.wait_recv()
    for i in range(HH):
        finish(other0 + i, qbr1[i * HD : (i + 1) * HD, :])
    put(other0, 5)
    for copy in outs:
        copy.wait()

    for copy in (pair0, post0, pair1, post1):
        copy.wait_send()
    drain(fbuf0, C - 1, ssem.at[1])
    drain(sbuf0, C - 1, ssem.at[2])
    drain(zbuf, Z - 1, ssem.at[4])
    drain(fbuf1, C - 1, ssem.at[6])
    drain(gbuf, RW - 1, ssem.at[7])
    drain(sbuf1, C - 1, ssem.at[8])
    drain(cbuf, CW - 1, ssem.at[9])


def mover(parts, *refs):
    half = len(parts)
    srcs, dsts, held = refs[:half], refs[half : 2 * half], refs[2 * half : 3 * half]
    sin, sout = refs[3 * half :]
    ins, outs = [], []
    for i in range(half):
        step = srcs[i].shape[0] // parts[i]
        for j in range(parts[i]):
            piece = pl.ds(j * step, step)
            slot = len(ins)
            ins.append(pltpu.make_async_copy(srcs[i].at[piece], held[i].at[piece], sin.at[slot]))
            outs.append(pltpu.make_async_copy(held[i].at[piece], dsts[i].at[piece], sout.at[slot]))
    for copy in ins:
        copy.start()
    for a, b in zip(ins, outs):
        a.wait()
        b.start()
    for copy in outs:
        copy.wait()


def body(queries, keys, values, gate, grad_out, gain, decay_rate, segment_ids):
    R = lax.axis_size("ctx")
    Z = lax.axis_size("head")
    T, W = queries.shape
    H = W // HD
    N = T // BLOCK
    RW = 8 if R == 32 else R // 2
    CW = R // RW
    C = R // 2
    HR = H * HD // 2
    SR = HR // C
    hbm = pl.BlockSpec(memory_space=pltpu.HBM)
    big = jax.ShapeDtypeStruct((T, W), BF16)
    small = jax.ShapeDtypeStruct((1, W), F32)
    VM = pltpu.VMEM
    scratch = (
        [VM((T, W), BF16)] * 4
        + [VM((1, W), F32)]
        + [VM((T, W), BF16)] * 5
        + [VM((1, W), F32), pltpu.SMEM((H,), F32), VM((1, T), jnp.int32)]
        + [
            VM((T, HD), F32),
            VM((H, BLOCK, HD), F32),
            VM((H, BLOCK, HD), F32),
            VM((H, BLOCK, BLOCK), F32),
            VM((N, H, HD, HD), F32),
            VM((N, H, BLOCK, BLOCK), BF16),
            VM((T, W), F32),
            VM((T, W), F32),
            VM((N, H, HD, HD), BF16),
            VM((BLOCK, 2 * N * HD), F32),
            VM((N, H, HD, BLOCK), BF16),
            VM((T, W), BF16),
            VM((N, H, HD, HD), F32),
            VM((T, W), F32),
            VM((T, W), F32),
            VM((T, HD), F32),
            VM((T, HD), F32),
        ]
        + [VM((HR + 8, HD), F32)] * 2
        + [VM((HR, HD), F32)] * 2
        + [VM((C, SR + 2, HD), F32)] * 2
        + [VM((C, SR, HD), F32)] * 2
        + [VM((HR, HD), F32)] * 2
        + [VM((HR, HD), F32)] * 3
        + [VM((C, SR, HD), F32)] * 4
        + [VM((HR, HD), F32)] * 2
        + [
            VM((N, 1, HD), F32),
            VM((N, 1, HD), F32),
            VM((Z, 2 * N, BLOCK), F32),
            VM((RW, 1, W), F32),
            VM((CW, 1, W), F32),
            pltpu.SemaphoreType.DMA((8,)),
            pltpu.SemaphoreType.DMA((7,)),
            pltpu.SemaphoreType.DMA((11,)),
            pltpu.SemaphoreType.DMA((11,)),
        ]
    )
    outs = pl.pallas_call(
        functools.partial(kernel, (R, Z, RW, N, H)),
        out_shape=(big, big, big, big, small),
        in_specs=[hbm] * 8,
        out_specs=(hbm,) * 5,
        scratch_shapes=scratch,
        compiler_params=pltpu.CompilerParams(
            collective_id=0, has_side_effects=True, vmem_limit_bytes=VMEM_A
        ),
    )(
        queries, keys, values, gate, grad_out,
        gain.reshape(1, W), decay_rate, segment_ids.reshape(1, T),
    )
    parts = (2, 2, 2, 2, 1)
    moved = pl.pallas_call(
        functools.partial(mover, parts),
        out_shape=(big, big, big, big, small),
        in_specs=[hbm] * 5,
        out_specs=(hbm,) * 5,
        scratch_shapes=[VM((T, W), BF16)] * 4
        + [VM((1, W), F32)]
        + [pltpu.SemaphoreType.DMA((sum(parts),))] * 2,
        compiler_params=pltpu.CompilerParams(vmem_limit_bytes=VMEM_A),
    )(*outs)
    dq, dk, dv, gg, dgain = moved
    return dq, dk, dv, gg, dgain.reshape(W)


def solution(mesh):
    in_specs = (P("ctx", "head"),) * 5 + (P("head"), P("head"), P("ctx"))
    out_specs = (P("ctx", "head"),) * 4 + (P("head"),)
    return jax.shard_map(body, mesh=mesh, in_specs=in_specs, out_specs=out_specs, check_vma=False)
```

time: 54.1 us -> 49.3 us (0.911)
  local copies, waits for them, and re-layouts: 7.7 us -> 0 us
  Pallas kernels: 45.4 us -> 48.6 us
    unnamed x17 -> x0, local copies, waits for them, and re-layouts: 7.7 us -> none
    pallas_call x0 -> x1, Pallas kernels: none -> 3.6 us  [body(): pl.pallas_call(functools.partial(mover, parts), out_shape=(big, big, big,...]
where the time goes in v2:
time: 49.3 us; the launch traced here: 49.2 us
  Pallas kernels  48.6 us (99%)
  between operations  0.64 us (1%)
    pallas_call x1, Pallas kernels, body(): pl.pallas_call(functools.partial(kernel, (R, Z, RW, N, H)), out_shape=(bi...  45 us
    pallas_call x1, Pallas kernels, body(): pl.pallas_call(functools.partial(mover, parts), out_shape=(big, big, big,...  3.6 us

profile of v2, /device:TPU:1, one launch (start us, length us, event | category | flops | bytes accessed | tf_op | source)
XLA Modules:
  0.0 49.2 jit_solution(15330708584727209924)
XLA Ops:
  0.6 45.0 %shard_map.119 = (bf16[1024,512]{1,0:T(8,128)(2,1)}, bf16[1024,512]{1,0:T(8,128)(2,1)}, bf16[1024,512]{1,0:T(8,128)(2,1)}, bf16[1024,512]{1,0:T(8,128)(2,1)}, f32[1,512]{1,0:T(1,128)}) custom-call(bf16[1024,512]{1,0:T(8,128)(2,1)} %q_hbm.1, bf16[1024,512]{1,0:T(8,128)(2,1)} %k_hbm.1, bf16[1024,512]{1,0:T(8,128)(2,1)} %v_hbm.1, bf16[1024,512]{1,0:T(8,128)(2,1)} %g_hbm.1, ...), custom_call_target="tpu_custom_call" | custom-call | tf_op jit(solution)/shard_map/pallas_call | solution.py:586
  45.6 3.6 %shard_map.120 = (bf16[1024,512]{1,0:T(8,128)(2,1)}, bf16[1024,512]{1,0:T(8,128)(2,1)}, bf16[1024,512]{1,0:T(8,128)(2,1)}, bf16[1024,512]{1,0:T(8,128)(2,1)}, f32[1,512]{1,0:T(1,128)}) custom-call(bf16[1024,512]{1,0:T(8,128)(2,1)} %get-tuple-element.15.refs_0_, bf16[1024,512]{1,0:T(8,128)(2,1)} %get-tuple-element.16.refs_1_, ...), custom_call_target="tpu_custom_call" | custom-call | tf_op jit(solution)/shard_map/pallas_call | solution.py:600

commit v3 on v2

--- a/solution.py
+++ b/solution.py
@@ -13,7 +13,8 @@
 BLOCK = 256
 HD = 128
 EPS = 1e-06
-VMEM_A = 56 * 1024 * 1024
+VMEM_A = 49 * 1024 * 1024
+VMEM_B = 8 * 1024 * 1024
 
 
 def nn(a, b):
@@ -29,6 +30,8 @@
 
 
 def drain(ref, count, sem):
+    if count == 0:
+        return
     part = ref.at[pl.ds(0, count)]
     pltpu.make_async_copy(part, part, sem).wait()
 
@@ -36,23 +39,23 @@
 def kernel(
     dims,
     q_hbm, k_hbm, v_hbm, g_hbm, o_hbm, gain_hbm, rate_hbm, seg_hbm,
-    dq_hbm, dk_hbm, dv_hbm, gg_hbm, dgain_hbm,
-    dqv, dkv, dvv, ggv, dgain_ref, qv, kv, vv, gv, ov, gain_ref, rate_ref, seg_ref,
-    segc, wl, wf, wb, fst, sw, attn, gs, sst, bc, qwt, datt, rst, dkp, dvp, ssq, sda,
+    dqv, dkv, dvv, ggv, dgain_ref,
+    qv, kv, vv, gv, ov, gain_ref, rate_ref, seg_ref,
+    segc, wl, wf, wb, fst, sw, attn, dzs, sst, bc, qwt, datt, rst, dkp, dvp, ssq, sda, qc, pows,
     pbs0, pbr0, hfs, fen, fbuf0, rbuf0, sbuf0, ebuf0, qbs0, qbr0,
     pbs1, pbr1, fen1, fbuf1, rbuf1, sbuf1, ebuf1, qbs1, qbr1,
     flab, rlab, zbuf, gbuf, cbuf,
-    in_sem, out_sem, ssem, rsem,
+    in_sem, ssem, rsem,
 ):
     R, Z, RW, N, H = dims
     T = N * BLOCK
     C = R // 2
     HH = H // 2
     HR = HH * HD
-    SR = HR // C
-    HJ = C // HH
+    CX = 4
+    SR = HR // CX
+    HJ = CX // HH
     CW = R // RW
-    CX = 4
     CY = C // CX
     me = lax.axis_index("ctx")
     zme = lax.axis_index("head")
@@ -123,19 +126,15 @@
     loads[1].wait()
     for h in range(H):
         wl[h] = jnp.exp(-rate_ref[h] * (BLOCK - 1.0 - iota))
+        for i, times in enumerate((1.0, float(BLOCK), float(T), 2.0 * T)):
+            pows[i, h] = power(h, times)
     mylast = segc[T - 1 : T, :]
     myfirst = segc[0:1, :]
 
-    def reach(o):
-        return min(o[0], CY - o[0]) + min(o[1], CX - o[1])
-
-    offsets = sorted(
-        ((dy, dx) for dy in range(CY) for dx in range(CX) if dy or dx), key=reach, reverse=True
-    )
-
-    def each_chip(send):
-        for dy, dx in offsets:
-            send(lax.rem(chipy + dy, CY) * CX + lax.rem(chipx + dx, CX))
+    def at_chip(y, x):
+        return 2 * (y * CX + x) + core
+
+    around = (2, 1, 3)
 
     def merge(entry, pbr, lab_m, lab_p, fen_ref, fbuf):
         is_entry = core == entry
@@ -148,7 +147,7 @@
             fe = lax.select(is_entry, fm, fp)
             fx = lax.select(is_entry, fp, fm)
             fen_ref[part, :] = fe
-            c = fx + jnp.where(lab_entry == lab_exit, power(own0 + i, float(T)), 0.0) * fe
+            c = fx + jnp.where(lab_entry == lab_exit, pows[2, own0 + i], 0.0) * fe
             fbuf[i * HJ : (i + 1) * HJ, 0:SR, :] = c.reshape(HJ, SR, HD)
         return lab_entry, lab_exit
 
@@ -158,15 +157,15 @@
         for i in range(HH):
             part = slice(i * HD, (i + 1) * HD)
             ve = ebuf[i * HJ : (i + 1) * HJ].reshape(HD, HD)
-            linked = jnp.where(lab_in == lab_entry, power(own0 + i, float(T)), 0.0)
+            linked = jnp.where(lab_in == lab_entry, pows[2, own0 + i], 0.0)
             vx = fen_ref[part, :] + linked * ve
             qbs[part, :] = lax.select(is_entry, vx, ve)
             kept.append(lax.select(is_entry, ve, vx))
-        return kept, lax.select(is_entry, lab_in, lab_entry)
+        return kept
 
     def device_state(h):
         own = None
-        pb = power(h, float(BLOCK))
+        pb = pows[1, h]
         w = wl[h]
         for n in range(N):
             last = segc[n * BLOCK + BLOCK - 1 : n * BLOCK + BLOCK, :]
@@ -196,25 +195,26 @@
     matelast = pbr0[HR : HR + 1, :]
     matefirst = pbr0[HR + 1 : HR + 2, :]
     lab_entry0, lab_exit0 = merge(0, pbr0, mylast, matelast, fen, fbuf0)
-    chipfirst = lax.select(core == 0, myfirst, matefirst)
-    for c in range(C):
-        fbuf0[c, SR : SR + 2, :] = jnp.concatenate([lab_exit0, chipfirst], axis=0)
-
-    def scatter(fbuf, rbuf, phase):
-        def send(c):
-            remote(fbuf.at[c], rbuf.at[chip], phase, 2 * c + core, zme).start()
-
-        each_chip(send)
-        rbuf[chip] = fbuf[chip]
+    for x in range(CX):
+        fbuf0[x, SR : SR + 1, :] = lab_exit0
+
+    def scatter(fbuf, rbuf, phase, turn_y, near, far):
+        there = lax.rem(chipy + turn_y, CY)
+        for dx in (2, 1, 3, 0):
+            x = lax.rem(chipx + dx, CX)
+            remote(fbuf.at[x], rbuf.at[far + chipx], phase, at_chip(there, x), zme).start()
+        for dx in around:
+            x = lax.rem(chipx + dx, CX)
+            remote(fbuf.at[x], rbuf.at[near + chipx], phase, at_chip(chipy, x), zme).start()
+        rbuf[near + chipx] = fbuf[chipx]
 
     def spread(sbuf, ebuf, phase):
-        def send(c):
-            remote(sbuf.at[c], ebuf.at[chip], phase, 2 * c + core, zme).start()
-
-        each_chip(send)
-        ebuf[chip] = sbuf[chip]
-
-    scatter(fbuf0, rbuf0, 1)
+        for dx in around:
+            x = lax.rem(chipx + dx, CX)
+            remote(sbuf.at[x], ebuf.at[chipx], phase, at_chip(chipy, x), zme).start()
+        ebuf[chipx] = sbuf[chipx]
+
+    scatter(fbuf0, rbuf0, 1, 1, CX, 0)
 
     d2 = (
         lax.broadcasted_iota(jnp.int32, (BLOCK, BLOCK), 0)
@@ -236,32 +236,43 @@
             sw[n, h] = s
             attn[rows(n), col(h)] = nn(s, vv[rows(n), col(h)])
             sig = jax.nn.sigmoid(gv[rows(n), col(h)].astype(F32))
-            gs[rows(n), col(h)] = ov[rows(n), col(h)].astype(F32) * sig
+            dzs[rows(n), col(h)] = ov[rows(n), col(h)].astype(F32) * sig * gain_ref[0:1, col(h)]
         return c
 
     for copy in loads[4:]:
         copy.wait()
     lax.fori_loop(0, N // 2, intra, 0)
 
-    hold = own0 + chip // HJ
-    pchip = power(hold, 2.0 * T)
-    drain(rbuf0, C - 1, rsem.at[1])
-    acc = jnp.zeros((SR, HD), F32)
-    for c in range(C - 1):
-        sbuf0[c] = acc
-        if c == 0:
-            acc = rbuf0[c, 0:SR, :]
-        else:
-            linked = rbuf0[c - 1, SR : SR + 1, :] == rbuf0[c, SR : SR + 1, :]
-            acc = rbuf0[c, 0:SR, :] + jnp.where(linked, pchip, 0.0) * acc
-    sbuf0[C - 1] = acc
+    pchip = pows[3, own0 + chipx // HJ]
+    drain(rbuf0, 2 * CX - 1, rsem.at[1])
+    acc = rbuf0[0, 0:SR, :]
+    for i in range(1, 2 * CX):
+        if i >= CX:
+            sbuf0[i - CX] = acc
+        if i < 2 * CX - 1:
+            linked = rbuf0[i - 1, SR : SR + 1, :] == rbuf0[i, SR : SR + 1, :]
+            acc = rbuf0[i, 0:SR, :] + jnp.where(linked, pchip, 0.0) * acc
     spread(sbuf0, ebuf0, 2)
 
+    lab_in0 = rbuf0[CX - 1 + chipx, SR : SR + 1, :]
+    flab[0] = lax.select(core == 0, lab_in0, lab_entry0)
+    for n in range(1, N):
+        flab[n] = segc[n * BLOCK - 1 : n * BLOCK, :]
+        rlab[n - 1] = segc[n * BLOCK : n * BLOCK + 1, :]
+
+    def decayed(n, c):
+        linked = segc[rows(n), :] == flab[n]
+        for h in range(H):
+            qd = jnp.where(linked, qv[rows(n), col(h)].astype(F32) * wf[h], 0.0)
+            qc[rows(n), col(h)] = qd.astype(BF16)
+        return c
+
     lax.fori_loop(N // 2, N, intra, 0)
+    lax.fori_loop(0, N, decayed, 0)
 
     def chain(h, incoming):
-        lam = power(h, 1.0)
-        pb = power(h, float(BLOCK))
+        lam = pows[0, h]
+        pb = pows[1, h]
         state = lam * incoming
         for n in range(N):
             sst[n, h] = state.astype(BF16)
@@ -272,16 +283,14 @@
     row16 = lax.broadcasted_iota(jnp.int32, (16, HD), 0)
 
     def cross(n, h0):
-        linked = segc[rows(n), :] == flab[n]
         sq = jnp.zeros((BLOCK, HD), F32)
         da = jnp.zeros((BLOCK, HD), F32)
         for i in range(HH):
             h = h0 + i
-            c = nn(qv[rows(n), col(h)], sst[n, h])
-            a = attn[rows(n), col(h)] + jnp.where(linked, wf[h], 0.0) * c
+            a = attn[rows(n), col(h)] + nn(qc[rows(n), col(h)], sst[n, h])
             attn[rows(n), col(h)] = a
             sq = sq + a * a
-            da = da + (gs[rows(n), col(h)] * gain_ref[0:1, col(h)]) * a
+            da = da + dzs[rows(n), col(h)] * a
         return sq, da
 
     def cross_own(n, c):
@@ -298,13 +307,8 @@
         da = (da + sda[rows(n), :]).astype(BF16)
         return total + nt(pick1, sq) + nt(pick2, da)
 
-    lab_in0 = rbuf0[jnp.maximum(chip - 1, 0), SR : SR + 1, :]
-    for n in range(1, N):
-        flab[n] = segc[n * BLOCK - 1 : n * BLOCK, :]
-        rlab[n - 1] = segc[n * BLOCK : n * BLOCK + 1, :]
-    drain(ebuf0, C - 1, rsem.at[2])
-    kept, label = hand_over(0, fen, ebuf0, lab_entry0, lab_in0, qbs0)
-    flab[0] = label
+    drain(ebuf0, CX - 1, rsem.at[2])
+    kept = hand_over(0, fen, ebuf0, lab_entry0, lab_in0, qbs0)
     post0 = remote(qbs0, qbr0, 3, mate, zme)
     post0.start()
     for i in range(HH):
@@ -353,10 +357,9 @@
 
     def reverse_state(h):
         own = None
-        pb = power(h, float(BLOCK))
+        pb = pows[1, h]
         for n in reversed(range(N)):
-            dz = gs[rows(n), col(h)] * gain_ref[0:1, col(h)]
-            d = (factor(n) * dz - factor(N + n) * attn[rows(n), col(h)]).astype(BF16)
+            d = (factor(n) * dzs[rows(n), col(h)] - factor(N + n) * attn[rows(n), col(h)]).astype(BF16)
             datt[rows(n), col(h)] = d
             f = nn(qwt[n, h], d)
             rst[n, h] = f
@@ -375,15 +378,17 @@
     for i in range(HH):
         hfs[i * HD : (i + 1) * HD, :] = reverse_state(own0 + i)
     pair1.wait_recv()
-    lab_entry1, _ = merge(1, pbr1, myfirst, matefirst, fen1, fbuf1)
-    scatter(fbuf1, rbuf1, 6)
+    lab_entry1, lab_exit1 = merge(1, pbr1, myfirst, matefirst, fen1, fbuf1)
+    for x in range(CX):
+        fbuf1[x, SR : SR + 1, :] = lab_exit1
+    scatter(fbuf1, rbuf1, 6, CY - 1, 0, CX)
 
     def gated(n, sums):
         out = []
         for h in range(H):
             normed = attn[rows(n), col(h)] * factor(n)
-            t = gs[rows(n), col(h)] * normed
             sig = jax.nn.sigmoid(gv[rows(n), col(h)].astype(F32))
+            t = ov[rows(n), col(h)].astype(F32) * sig * normed
             ggv[rows(n), col(h)] = (t * gain_ref[0:1, col(h)] * (1.0 - sig)).astype(BF16)
             out.append(sums[h] + jnp.sum(t.reshape(BLOCK // 8, 8, HD), axis=0))
         return tuple(out)
@@ -396,8 +401,6 @@
         return c
 
     lax.fori_loop(1, RW, gain_row, 0)
-    out_gg = pltpu.make_async_copy(ggv, gg_hbm, out_sem.at[0])
-    out_gg.start()
 
     def back(n, c):
         same = same_of(n)
@@ -415,16 +418,14 @@
 
     lax.fori_loop(0, N // 2, back, 0)
 
-    drain(rbuf1, C - 1, rsem.at[6])
-    acc = jnp.zeros((SR, HD), F32)
-    for c in reversed(range(1, C)):
-        sbuf1[c] = acc
-        if c == C - 1:
-            acc = rbuf1[c]
-        else:
-            linked = rbuf0[c + 1, SR + 1 : SR + 2, :] == rbuf0[c, SR + 1 : SR + 2, :]
-            acc = rbuf1[c] + jnp.where(linked, pchip, 0.0) * acc
-    sbuf1[0] = acc
+    drain(rbuf1, 2 * CX - 1, rsem.at[6])
+    acc = rbuf1[2 * CX - 1, 0:SR, :]
+    for i in reversed(range(2 * CX - 1)):
+        if i < CX:
+            sbuf1[i] = acc
+        if i > 0:
+            linked = rbuf1[i + 1, SR : SR + 1, :] == rbuf1[i, SR : SR + 1, :]
+            acc = rbuf1[i, 0:SR, :] + jnp.where(linked, pchip, 0.0) * acc
     spread(sbuf1, ebuf1, 8)
 
     drain(gbuf, RW - 1, rsem.at[7])
@@ -441,20 +442,16 @@
     lax.fori_loop(1, CW, gain_col, 0)
 
     lax.fori_loop(N // 2, N, back, 0)
-    out_dq = pltpu.make_async_copy(dqv, dq_hbm, out_sem.at[1])
-    out_dq.start()
 
     drain(cbuf, CW - 1, rsem.at[9])
     part = cbuf[0]
     for i in range(1, CW):
         part = part + cbuf[i]
     dgain_ref[...] = part
-    out_gain = pltpu.make_async_copy(dgain_ref, dgain_hbm, out_sem.at[2])
-    out_gain.start()
 
     def finish(h, incoming):
-        lam = power(h, 1.0)
-        pb = power(h, float(BLOCK))
+        lam = pows[0, h]
+        pb = pows[1, h]
         state = lam * incoming
         for n in reversed(range(N)):
             rin = state.astype(BF16)
@@ -467,60 +464,37 @@
                 keep = rlab[n] == rlab[n - 1]
                 state = jnp.where(keep, pb, 0.0) * state + lam * rst[n, h]
 
-    lab_in1 = rbuf0[jnp.minimum(chip + 1, C - 1), SR + 1 : SR + 2, :]
-    drain(ebuf1, C - 1, rsem.at[8])
-    kept, label = hand_over(1, fen1, ebuf1, lab_entry1, lab_in1, qbs1)
-    rlab[N - 1] = label
+    lab_in1 = rbuf1[chipx + 1, SR : SR + 1, :]
+    drain(ebuf1, CX - 1, rsem.at[8])
+    kept = hand_over(1, fen1, ebuf1, lab_entry1, lab_in1, qbs1)
+    rlab[N - 1] = lax.select(core == 1, lab_in1, lab_entry1)
     post1 = remote(qbs1, qbr1, 10, mate, zme)
     post1.start()
-    outs = [out_gg, out_dq, out_gain]
-
-    def put(h0, slot):
-        part = pl.ds(pl.multiple_of(h0 * HD, HD), HH * HD)
-        for i, (src, dst) in enumerate(((dkv, dk_hbm), (dvv, dv_hbm))):
-            copy = pltpu.make_async_copy(src.at[:, part], dst.at[:, part], out_sem.at[slot + i])
-            copy.start()
-            outs.append(copy)
-
     for i in range(HH):
         finish(own0 + i, kept[i])
-    put(own0, 3)
     post1.wait_recv()
     for i in range(HH):
         finish(other0 + i, qbr1[i * HD : (i + 1) * HD, :])
-    put(other0, 5)
-    for copy in outs:
-        copy.wait()
-
     for copy in (pair0, post0, pair1, post1):
         copy.wait_send()
-    drain(fbuf0, C - 1, ssem.at[1])
-    drain(sbuf0, C - 1, ssem.at[2])
+    drain(rbuf0, 2 * CX - 1, ssem.at[1])
+    drain(sbuf0, CX - 1, ssem.at[2])
     drain(zbuf, Z - 1, ssem.at[4])
-    drain(fbuf1, C - 1, ssem.at[6])
+    drain(rbuf1, 2 * CX - 1, ssem.at[6])
     drain(gbuf, RW - 1, ssem.at[7])
-    drain(sbuf1, C - 1, ssem.at[8])
+    drain(sbuf1, CX - 1, ssem.at[8])
     drain(cbuf, CW - 1, ssem.at[9])
 
 
-def mover(parts, *refs):
-    half = len(parts)
-    srcs, dsts, held = refs[:half], refs[half : 2 * half], refs[2 * half : 3 * half]
-    sin, sout = refs[3 * half :]
-    ins, outs = [], []
-    for i in range(half):
-        step = srcs[i].shape[0] // parts[i]
-        for j in range(parts[i]):
-            piece = pl.ds(j * step, step)
-            slot = len(ins)
-            ins.append(pltpu.make_async_copy(srcs[i].at[piece], held[i].at[piece], sin.at[slot]))
-            outs.append(pltpu.make_async_copy(held[i].at[piece], dsts[i].at[piece], sout.at[slot]))
-    for copy in ins:
+def mover(*refs):
+    half = len(refs) // 2
+    sems = refs[-1]
+    copies = [
+        pltpu.make_async_copy(refs[i], refs[half + i], sems.at[i]) for i in range(half)
+    ]
+    for copy in copies:
         copy.start()
-    for a, b in zip(ins, outs):
-        a.wait()
-        b.start()
-    for copy in outs:
+    for copy in copies:
         copy.wait()
 
 
@@ -532,17 +506,16 @@
     N = T // BLOCK
     RW = 8 if R == 32 else R // 2
     CW = R // RW
-    C = R // 2
+    CX = 4
     HR = H * HD // 2
-    SR = HR // C
+    SR = HR // CX
     hbm = pl.BlockSpec(memory_space=pltpu.HBM)
+    vspec = pl.BlockSpec(memory_space=pltpu.VMEM)
     big = jax.ShapeDtypeStruct((T, W), BF16)
     small = jax.ShapeDtypeStruct((1, W), F32)
     VM = pltpu.VMEM
     scratch = (
-        [VM((T, W), BF16)] * 4
-        + [VM((1, W), F32)]
-        + [VM((T, W), BF16)] * 5
+        [VM((T, W), BF16)] * 5
         + [VM((1, W), F32), pltpu.SMEM((H,), F32), VM((1, T), jnp.int32)]
         + [
             VM((T, HD), F32),
@@ -562,14 +535,18 @@
             VM((T, W), F32),
             VM((T, HD), F32),
             VM((T, HD), F32),
+            VM((T, W), BF16),
+            VM((4, H, 1, HD), F32),
         ]
         + [VM((HR + 8, HD), F32)] * 2
         + [VM((HR, HD), F32)] * 2
-        + [VM((C, SR + 2, HD), F32)] * 2
-        + [VM((C, SR, HD), F32)] * 2
+        + [VM((CX, SR + 8, HD), F32), VM((2 * CX, SR + 8, HD), F32)]
+        + [VM((CX, SR, HD), F32)] * 2
         + [VM((HR, HD), F32)] * 2
-        + [VM((HR, HD), F32)] * 3
-        + [VM((C, SR, HD), F32)] * 4
+        + [VM((HR + 8, HD), F32)] * 2
+        + [VM((HR, HD), F32)]
+        + [VM((CX, SR + 8, HD), F32), VM((2 * CX, SR + 8, HD), F32)]
+        + [VM((CX, SR, HD), F32)] * 2
         + [VM((HR, HD), F32)] * 2
         + [
             VM((N, 1, HD), F32),
@@ -578,7 +555,6 @@
             VM((RW, 1, W), F32),
             VM((CW, 1, W), F32),
             pltpu.SemaphoreType.DMA((8,)),
-            pltpu.SemaphoreType.DMA((7,)),
             pltpu.SemaphoreType.DMA((11,)),
             pltpu.SemaphoreType.DMA((11,)),
         ]
@@ -587,7 +563,7 @@
         functools.partial(kernel, (R, Z, RW, N, H)),
         out_shape=(big, big, big, big, small),
         in_specs=[hbm] * 8,
-        out_specs=(hbm,) * 5,
+        out_specs=(vspec,) * 5,
         scratch_shapes=scratch,
         compiler_params=pltpu.CompilerParams(
             collective_id=0, has_side_effects=True, vmem_limit_bytes=VMEM_A
@@ -596,16 +572,13 @@
         queries, keys, values, gate, grad_out,
         gain.reshape(1, W), decay_rate, segment_ids.reshape(1, T),
     )
-    parts = (2, 2, 2, 2, 1)
     moved = pl.pallas_call(
-        functools.partial(mover, parts),
+        mover,
         out_shape=(big, big, big, big, small),
-        in_specs=[hbm] * 5,
+        in_specs=[vspec] * 5,
         out_specs=(hbm,) * 5,
-        scratch_shapes=[VM((T, W), BF16)] * 4
-        + [VM((1, W), F32)]
-        + [pltpu.SemaphoreType.DMA((sum(parts),))] * 2,
-        compiler_params=pltpu.CompilerParams(vmem_limit_bytes=VMEM_A),
+        scratch_shapes=[pltpu.SemaphoreType.DMA((5,))],
+        compiler_params=pltpu.CompilerParams(vmem_limit_bytes=VMEM_B),
     )(*outs)
     dq, dk, dv, gg, dgain = moved
     return dq, dk, dv, gg, dgain.reshape(W)

time: 49.3 us -> 47.2 us (0.957)
  Pallas kernels: 48.6 us -> 45 us
  local copies, waits for them, and re-layouts: 0 us -> 1.36 us
    pallas_call x1, Pallas kernels: 45 us -> 42.9 us  [body(): pl.pallas_call(functools.partial(kernel, (R, Z, RW, N, H)), out_shape=(bi...]
    pallas_call x1, Pallas kernels: 3.6 us -> 2.05 us  [body(): pl.pallas_call(mover, out_shape=(big, big, big, big, small), in_specs=[vs...]
    unnamed x0 -> x6, local copies, waits for them, and re-layouts: none -> 1.36 us
where the time goes in v3:
time: 47.2 us; the launch traced here: 47 us
  Pallas kernels  45 us (95%)
  local copies, waits for them, and re-layouts  1.36 us (3%)
  between operations  0.66 us (1%)
    pallas_call x1, Pallas kernels, body(): pl.pallas_call(functools.partial(kernel, (R, Z, RW, N, H)), out_shape=(bi...  42.9 us
    pallas_call x1, Pallas kernels, body(): pl.pallas_call(mover, out_shape=(big, big, big, big, small), in_specs=[vs...  2.05 us
    unnamed x6, local copies, waits for them, and re-layouts  1.36 us

profile of v3, /device:TPU:1, one launch (start us, length us, event | category | flops | bytes accessed | tf_op | source)
XLA Modules:
  0.0 47.0 jit_solution(14780963071450453487)
XLA Ops:
  0.6 0.0 copy-start.1
  0.6 0.0 copy-start.2
  0.7 0.7 %copy-done.1 = f32[512]{0:T(512)S(1)} copy-done((f32[512]{0:T(512)S(1)}, f32[512]{0:T(512)}, u32[]{:S(2)}) %copy-start.1) | copy-done | bytes 2072
  1.3 0.0 copy-done.2
  1.3 0.0 copy-start
  1.3 0.7 %copy-done = s32[1024]{0:T(1024)S(1)} copy-done((s32[1024]{0:T(1024)S(1)}, s32[1024]{0:T(1024)}, u32[]{:S(2)}) %copy-start) | copy-done | bytes 4120
  2.0 42.9 %shard_map.119 = (bf16[1024,512]{1,0:T(8,128)(2,1)S(1)}, bf16[1024,512]{1,0:T(8,128)(2,1)S(1)}, bf16[1024,512]{1,0:T(8,128)(2,1)S(1)}, bf16[1024,512]{1,0:T(8,128)(2,1)S(1)}, f32[1,512]{1,0:T(1,128)S(1)}) custom-call(bf16[1024,512]{1,0:T(8,128)(2,1)} %q_hbm.1, bf16[1024,512]{1,0:T(8,128)(2,1)} %k_hbm.1, bf16[1024,512]{1,0:T(8,128)(2,1)} %v_hbm.1, ...), custom_call_target="tpu_custom_call" | custom-call | tf_op jit(solution)/shard_map/pallas_call | solution.py:562
  45.0 2.1 %shard_map.120 = (bf16[1024,512]{1,0:T(8,128)(2,1)}, bf16[1024,512]{1,0:T(8,128)(2,1)}, bf16[1024,512]{1,0:T(8,128)(2,1)}, bf16[1024,512]{1,0:T(8,128)(2,1)}, f32[1,512]{1,0:T(1,128)}) custom-call(bf16[1024,512]{1,0:T(8,128)(2,1)S(1)} %get-tuple-element.15.refs_0_, bf16[1024,512]{1,0:T(8,128)(2,1)S(1)} %get-tuple-element.16.refs_1_, ...), custom_call_target="tpu_custom_call" | custom-call | tf_op jit(solution)/shard_map/pallas_call | solution.py:575
Async XLA Ops:
  0.6 0.7 %copy-start.1 = (f32[512]{0:T(512)S(1)}, f32[512]{0:T(512)}, u32[]{:S(2)}) copy-start(f32[512]{0:T(512)} %param.13) | copy-start | bytes 6148
  0.6 0.7 %copy-start.2 = (f32[4]{0:T(128)S(1)}, f32[4]{0:T(128)}, u32[]{:S(2)}) copy-start(f32[4]{0:T(128)} %rate_hbm.1) | copy-start | bytes 52
  1.3 0.7 %copy-start = (s32[1024]{0:T(1024)S(1)}, s32[1024]{0:T(1024)}, u32[]{:S(2)}) copy-start(s32[1024]{0:T(1024)} %param.15) | copy-start | bytes 12292

commit v4 on v3

--- a/solution.py
+++ b/solution.py
@@ -38,16 +38,16 @@
 
 def kernel(
     dims,
-    q_hbm, k_hbm, v_hbm, g_hbm, o_hbm, gain_hbm, rate_hbm, seg_hbm,
+    q_hbm, k_hbm, v_hbm, g_hbm, o_hbm, small_hbm, seg_hbm,
     dqv, dkv, dvv, ggv, dgain_ref,
-    qv, kv, vv, gv, ov, gain_ref, rate_ref, seg_ref,
+    qv, kv, vv, gv, ov, small_ref, seg_ref,
     segc, wl, wf, wb, fst, sw, attn, dzs, sst, bc, qwt, datt, rst, dkp, dvp, ssq, sda, qc, pows,
     pbs0, pbr0, hfs, fen, fbuf0, rbuf0, sbuf0, ebuf0, qbs0, qbr0,
     pbs1, pbr1, fen1, fbuf1, rbuf1, sbuf1, ebuf1, qbs1, qbr1,
-    flab, rlab, zbuf, gbuf, cbuf,
+    flab, rlab, zbuf, gps, gpr, gbuf, cbuf,
     in_sem, ssem, rsem,
 ):
-    R, Z, RW, N, H = dims
+    R, Z, N, H = dims
     T = N * BLOCK
     C = R // 2
     HH = H // 2
@@ -55,13 +55,9 @@
     CX = 4
     SR = HR // CX
     HJ = CX // HH
-    CW = R // RW
     CY = C // CX
     me = lax.axis_index("ctx")
     zme = lax.axis_index("head")
-    row0 = (me // RW) * RW
-    mcol = me - row0
-    mrow = me // RW
     core = lax.rem(me, 2)
     mate = me + 1 - 2 * core
     chip = me // 2
@@ -74,8 +70,8 @@
         pltpu.make_async_copy(src, dst, in_sem.at[i])
         for i, (src, dst) in enumerate(
             (
-                (seg_hbm, seg_ref), (rate_hbm, rate_ref), (k_hbm, kv), (v_hbm, vv),
-                (q_hbm, qv), (g_hbm, gv), (o_hbm, ov), (gain_hbm, gain_ref),
+                (seg_hbm, seg_ref), (small_hbm, small_ref), (k_hbm, kv), (v_hbm, vv),
+                (q_hbm, qv), (g_hbm, gv), (o_hbm, ov),
             )
         )
     ]
@@ -87,16 +83,16 @@
     def greet(ctx, head):
         pl.semaphore_signal(barrier, inc=1, device_id=(ctx, head), device_id_type=MESH)
 
-    def greet_ctx(i, c):
-        greet(lax.rem(me + i, R), zme)
-        return c
-
-    def greet_head(i, c):
+    heads = sorted(range(1, Z), key=lambda i: min(i, Z - i), reverse=True)
+    near = {(dy, dx) for dy in (0, 1, CY - 1) for dx in range(CX)}
+    near = sorted((near | {(dy, 0) for dy in range(CY)}) - {(0, 0)}, reverse=True)
+    for i in heads:
         greet(me, lax.rem(zme + i, Z))
-        return c
-
-    lax.fori_loop(1, Z, greet_head, 0)
-    lax.fori_loop(1, R, greet_ctx, 0)
+    for dy, dx in near:
+        y, x = lax.rem(chipy + dy, CY), lax.rem(chipx + dx, CX)
+        greet(2 * (y * CX + x) + core, zme)
+    greet(mate, zme)
+    greeted = len(heads) + len(near) + 1
     for copy in loads[4:]:
         copy.start()
 
@@ -114,8 +110,14 @@
         start = n * BLOCK
         return pl.ds(start if isinstance(n, int) else pl.multiple_of(start, BLOCK), BLOCK)
 
+    def rate(h):
+        return small_ref[H + h : H + h + 1, :]
+
+    def gain(h):
+        return small_ref[h : h + 1, :]
+
     def power(h, times):
-        return jnp.exp(jnp.full((1, HD), -rate_ref[h] * times, F32))
+        return jnp.exp(rate(h) * -times)
 
     iota = lax.broadcasted_iota(jnp.int32, (BLOCK, HD), 0).astype(F32)
     first_row = jnp.where(lax.broadcasted_iota(jnp.int32, (16, HD), 0) == 0, 1.0, 0.0).astype(BF16)
@@ -125,7 +127,7 @@
         segc[rows(n), :] = tn(seg, first_row)
     loads[1].wait()
     for h in range(H):
-        wl[h] = jnp.exp(-rate_ref[h] * (BLOCK - 1.0 - iota))
+        wl[h] = jnp.exp(-rate(h) * (BLOCK - 1.0 - iota))
         for i, times in enumerate((1.0, float(BLOCK), float(T), 2.0 * T)):
             pows[i, h] = power(h, times)
     mylast = segc[T - 1 : T, :]
@@ -186,7 +188,7 @@
         pbs0[i * HD : (i + 1) * HD, :] = device_state(other0 + i)
     top = lax.broadcasted_iota(jnp.int32, (8, HD), 0) == 0
     pbs0[HR : HR + 8, :] = jnp.where(top, mylast, myfirst)
-    pl.semaphore_wait(barrier, R - 1 + Z - 1)
+    pl.semaphore_wait(barrier, greeted)
     pair0 = remote(pbs0, pbr0, 0, mate, zme)
     pair0.start()
     for i in range(HH):
@@ -221,8 +223,9 @@
         - lax.broadcasted_iota(jnp.int32, (BLOCK, BLOCK), 1)
     ).astype(F32)
     for h in range(H):
-        wf[h] = jnp.exp(-rate_ref[h] * iota)
-        wb[h] = jnp.where(d2 >= 0, jnp.exp(-rate_ref[h] * jnp.maximum(d2, 0.0)), 0.0)
+        wf[h] = jnp.exp(-rate(h) * iota)
+        rate2 = jnp.concatenate([rate(h), rate(h)], axis=1)
+        wb[h] = jnp.where(d2 >= 0, jnp.exp(-rate2 * jnp.maximum(d2, 0.0)), 0.0)
 
     def same_of(n):
         sc = segc[rows(n), :]
@@ -236,7 +239,7 @@
             sw[n, h] = s
             attn[rows(n), col(h)] = nn(s, vv[rows(n), col(h)])
             sig = jax.nn.sigmoid(gv[rows(n), col(h)].astype(F32))
-            dzs[rows(n), col(h)] = ov[rows(n), col(h)].astype(F32) * sig * gain_ref[0:1, col(h)]
+            dzs[rows(n), col(h)] = ov[rows(n), col(h)].astype(F32) * sig * gain(h)
         return c
 
     for copy in loads[4:]:
@@ -320,8 +323,7 @@
     total = lax.fori_loop(0, N, cross_other, jnp.zeros((16, BLOCK), F32))
     zbuf[zme] = total[0 : 2 * N, :]
 
-    zorder = sorted(range(1, Z), key=lambda i: min(i, Z - i), reverse=True)
-    for i in zorder:
+    for i in heads:
         remote(zbuf.at[zme], zbuf.at[zme], 4, me, lax.rem(zme + i, Z)).start()
 
     def turn(n, c):
@@ -389,18 +391,14 @@
             normed = attn[rows(n), col(h)] * factor(n)
             sig = jax.nn.sigmoid(gv[rows(n), col(h)].astype(F32))
             t = ov[rows(n), col(h)].astype(F32) * sig * normed
-            ggv[rows(n), col(h)] = (t * gain_ref[0:1, col(h)] * (1.0 - sig)).astype(BF16)
+            ggv[rows(n), col(h)] = (t * gain(h) * (1.0 - sig)).astype(BF16)
             out.append(sums[h] + jnp.sum(t.reshape(BLOCK // 8, 8, HD), axis=0))
         return tuple(out)
 
     sums = lax.fori_loop(0, N, gated, tuple(jnp.zeros((8, HD), F32) for _ in range(H)))
-    gbuf[mcol] = jnp.concatenate([jnp.sum(s, axis=0, keepdims=True) for s in sums], axis=1)
-
-    def gain_row(i, c):
-        remote(gbuf.at[mcol], gbuf.at[mcol], 7, row0 + lax.rem(mcol + i, RW), zme).start()
-        return c
-
-    lax.fori_loop(1, RW, gain_row, 0)
+    gps[...] = jnp.concatenate([jnp.sum(s, axis=0, keepdims=True) for s in sums], axis=1)
+    gain_pair = remote(gps, gpr, 11, mate, zme)
+    gain_pair.start()
 
     def back(n, c):
         same = same_of(n)
@@ -416,7 +414,13 @@
             dvp[rows(n), col(h)] = tn(sw[n, h], d)
         return c
 
-    lax.fori_loop(0, N // 2, back, 0)
+    lax.fori_loop(0, 1, back, 0)
+    gain_pair.wait_recv()
+    gbuf[chipx] = gps[...] + gpr[...]
+    for dx in around:
+        x = lax.rem(chipx + dx, CX)
+        remote(gbuf.at[chipx], gbuf.at[chipx], 7, at_chip(chipy, x), zme).start()
+    lax.fori_loop(1, N // 2, back, 0)
 
     drain(rbuf1, 2 * CX - 1, rsem.at[6])
     acc = rbuf1[2 * CX - 1, 0:SR, :]
@@ -428,24 +432,20 @@
             acc = rbuf1[i, 0:SR, :] + jnp.where(linked, pchip, 0.0) * acc
     spread(sbuf1, ebuf1, 8)
 
-    drain(gbuf, RW - 1, rsem.at[7])
+    drain(gbuf, CX - 1, rsem.at[7])
     part = gbuf[0]
-    for i in range(1, RW):
+    for i in range(1, CX):
         part = part + gbuf[i]
-    cbuf[mrow] = part
-
-    def gain_col(i, c):
-        other = lax.rem(mrow + i, CW)
-        remote(cbuf.at[mrow], cbuf.at[mrow], 9, other * RW + mcol, zme).start()
-        return c
-
-    lax.fori_loop(1, CW, gain_col, 0)
+    cbuf[chipy] = part
+    for dy in range(1, CY):
+        y = lax.rem(chipy + dy, CY)
+        remote(cbuf.at[chipy], cbuf.at[chipy], 9, at_chip(y, chipx), zme).start()
 
     lax.fori_loop(N // 2, N, back, 0)
 
-    drain(cbuf, CW - 1, rsem.at[9])
+    drain(cbuf, CY - 1, rsem.at[9])
     part = cbuf[0]
-    for i in range(1, CW):
+    for i in range(1, CY):
         part = part + cbuf[i]
     dgain_ref[...] = part
 
@@ -475,23 +475,27 @@
     post1.wait_recv()
     for i in range(HH):
         finish(other0 + i, qbr1[i * HD : (i + 1) * HD, :])
-    for copy in (pair0, post0, pair1, post1):
+    for copy in (pair0, post0, pair1, post1, gain_pair):
         copy.wait_send()
     drain(rbuf0, 2 * CX - 1, ssem.at[1])
     drain(sbuf0, CX - 1, ssem.at[2])
     drain(zbuf, Z - 1, ssem.at[4])
     drain(rbuf1, 2 * CX - 1, ssem.at[6])
-    drain(gbuf, RW - 1, ssem.at[7])
+    drain(gbuf, CX - 1, ssem.at[7])
     drain(sbuf1, CX - 1, ssem.at[8])
-    drain(cbuf, CW - 1, ssem.at[9])
-
-
-def mover(*refs):
+    drain(cbuf, CY - 1, ssem.at[9])
+
+
+def mover(pieces, *refs):
     half = len(refs) // 2
     sems = refs[-1]
-    copies = [
-        pltpu.make_async_copy(refs[i], refs[half + i], sems.at[i]) for i in range(half)
-    ]
+    copies = []
+    for i in range(half):
+        src, dst = refs[i], refs[half + i]
+        step = src.shape[0] // pieces[i]
+        for j in range(pieces[i]):
+            part = pl.ds(j * step, step)
+            copies.append(pltpu.make_async_copy(src.at[part], dst.at[part], sems.at[len(copies)]))
     for copy in copies:
         copy.start()
     for copy in copies:
@@ -504,8 +508,6 @@
     T, W = queries.shape
     H = W // HD
     N = T // BLOCK
-    RW = 8 if R == 32 else R // 2
-    CW = R // RW
     CX = 4
     HR = H * HD // 2
     SR = HR // CX
@@ -516,7 +518,7 @@
     VM = pltpu.VMEM
     scratch = (
         [VM((T, W), BF16)] * 5
-        + [VM((1, W), F32), pltpu.SMEM((H,), F32), VM((1, T), jnp.int32)]
+        + [VM((2 * H, HD), F32), VM((1, T), jnp.int32)]
         + [
             VM((T, HD), F32),
             VM((H, BLOCK, HD), F32),
@@ -552,17 +554,21 @@
             VM((N, 1, HD), F32),
             VM((N, 1, HD), F32),
             VM((Z, 2 * N, BLOCK), F32),
-            VM((RW, 1, W), F32),
-            VM((CW, 1, W), F32),
-            pltpu.SemaphoreType.DMA((8,)),
-            pltpu.SemaphoreType.DMA((11,)),
-            pltpu.SemaphoreType.DMA((11,)),
+            VM((1, W), F32),
+            VM((1, W), F32),
+            VM((CX, 1, W), F32),
+            VM((R // (2 * CX), 1, W), F32),
+            pltpu.SemaphoreType.DMA((7,)),
+            pltpu.SemaphoreType.DMA((12,)),
+            pltpu.SemaphoreType.DMA((12,)),
         ]
     )
+    rates = jnp.broadcast_to(decay_rate[:, None], (H, HD))
+    small_in = jnp.concatenate([gain.reshape(H, HD), rates], axis=0)
     outs = pl.pallas_call(
-        functools.partial(kernel, (R, Z, RW, N, H)),
+        functools.partial(kernel, (R, Z, N, H)),
         out_shape=(big, big, big, big, small),
-        in_specs=[hbm] * 8,
+        in_specs=[hbm] * 7,
         out_specs=(vspec,) * 5,
         scratch_shapes=scratch,
         compiler_params=pltpu.CompilerParams(
@@ -570,14 +576,15 @@
         ),
     )(
         queries, keys, values, gate, grad_out,
-        gain.reshape(1, W), decay_rate, segment_ids.reshape(1, T),
+        small_in, segment_ids.reshape(1, T),
     )
+    pieces = (4, 4, 4, 4, 1)
     moved = pl.pallas_call(
-        mover,
+        functools.partial(mover, pieces),
         out_shape=(big, big, big, big, small),
         in_specs=[vspec] * 5,
         out_specs=(hbm,) * 5,
-        scratch_shapes=[pltpu.SemaphoreType.DMA((5,))],
+        scratch_shapes=[pltpu.SemaphoreType.DMA((sum(pieces),))],
         compiler_params=pltpu.CompilerParams(vmem_limit_bytes=VMEM_B),
     )(*outs)
     dq, dk, dv, gg, dgain = moved

time: 47.2 us -> 46.5 us (0.985)
  Pallas kernels: 45 us -> 44.4 us
    pallas_call x2, Pallas kernels: 45 us -> 44.4 us  [the longest x1 42.2 us: body(): pl.pallas_call(functools.partial(kernel, (R, Z, N, H)), out_shape=(big, b...]
where the time goes in v4:
time: 46.5 us; the launch traced here: 46.4 us
  Pallas kernels  44.4 us (95%)
  local copies, waits for them, and re-layouts  1.25 us (3%)
  between operations  0.66 us (1%)
    pallas_call x1, Pallas kernels, body(): pl.pallas_call(functools.partial(kernel, (R, Z, N, H)), out_shape=(big, b...  42.2 us
    pallas_call x1, Pallas kernels, body(): pl.pallas_call(functools.partial(mover, pieces), out_shape=(big, big, big...  2.15 us
    unnamed x6, local copies, waits for them, and re-layouts  1.18 us

profile of v4, /device:TPU:1, one launch (start us, length us, event | category | flops | bytes accessed | tf_op | source)
XLA Modules:
  0.0 46.4 jit_solution(5343294119450105760)
XLA Ops:
  0.6 0.0 copy-start.2
  0.6 0.0 copy-start.1
  0.7 0.6 %copy-done.2 = f32[4]{0:T(128)S(1)} copy-done((f32[4]{0:T(128)S(1)}, f32[4]{0:T(128)}, u32[]{:S(2)}) %copy-start.2) | copy-done | bytes 40
  1.3 0.0 copy-start
  1.3 0.1 pad.1.clone
  1.4 0.0 copy-done.1
  1.4 0.1 pad_maximum_fusion.small_hbm
  1.4 0.5 %copy-done = s32[1024]{0:T(1024)S(1)} copy-done((s32[1024]{0:T(1024)S(1)}, s32[1024]{0:T(1024)}, u32[]{:S(2)}) %copy-start) | copy-done | bytes 4120
  2.0 42.2 %shard_map.119 = (bf16[1024,512]{1,0:T(8,128)(2,1)S(1)}, bf16[1024,512]{1,0:T(8,128)(2,1)S(1)}, bf16[1024,512]{1,0:T(8,128)(2,1)S(1)}, bf16[1024,512]{1,0:T(8,128)(2,1)S(1)}, f32[1,512]{1,0:T(1,128)S(1)}) custom-call(bf16[1024,512]{1,0:T(8,128)(2,1)} %q_hbm.1, bf16[1024,512]{1,0:T(8,128)(2,1)} %k_hbm.1, bf16[1024,512]{1,0:T(8,128)(2,1)} %v_hbm.1, ...), custom_call_target="tpu_custom_call" | custom-call | tf_op jit(solution)/shard_map/pallas_call | solution.py:568
  44.2 2.1 %shard_map.120 = (bf16[1024,512]{1,0:T(8,128)(2,1)}, bf16[1024,512]{1,0:T(8,128)(2,1)}, bf16[1024,512]{1,0:T(8,128)(2,1)}, bf16[1024,512]{1,0:T(8,128)(2,1)}, f32[1,512]{1,0:T(1,128)}) custom-call(bf16[1024,512]{1,0:T(8,128)(2,1)S(1)} %get-tuple-element.15.refs_0_, bf16[1024,512]{1,0:T(8,128)(2,1)S(1)} %get-tuple-element.16.refs_1_, ...), custom_call_target="tpu_custom_call" | custom-call | tf_op jit(solution)/shard_map/pallas_call | solution.py:582
Async XLA Ops:
  0.6 0.7 %copy-start.2 = (f32[4]{0:T(128)S(1)}, f32[4]{0:T(128)}, u32[]{:S(2)}) copy-start(f32[4]{0:T(128)} %param.14) | copy-start | bytes 52
  0.6 0.7 %copy-start.1 = (f32[512]{0:T(512)S(1)}, f32[512]{0:T(512)}, u32[]{:S(2)}) copy-start(f32[512]{0:T(512)} %param.13) | copy-start | bytes 6148
  1.3 0.7 %copy-start = (s32[1024]{0:T(1024)S(1)}, s32[1024]{0:T(1024)}, u32[]{:S(2)}) copy-start(s32[1024]{0:T(1024)} %param.15) | copy-start | bytes 12292

commit v5 on v4

--- a/solution.py
+++ b/solution.py
@@ -38,9 +38,9 @@
 
 def kernel(
     dims,
-    q_hbm, k_hbm, v_hbm, g_hbm, o_hbm, small_hbm, seg_hbm,
+    q_hbm, k_hbm, v_hbm, g_hbm, o_hbm, small_ref, seg_ref,
     dqv, dkv, dvv, ggv, dgain_ref,
-    qv, kv, vv, gv, ov, small_ref, seg_ref,
+    qv, kv, vv, gv, ov,
     segc, wl, wf, wb, fst, sw, attn, dzs, sst, bc, qwt, datt, rst, dkp, dvp, ssq, sda, qc, pows,
     pbs0, pbr0, hfs, fen, fbuf0, rbuf0, sbuf0, ebuf0, qbs0, qbr0,
     pbs1, pbr1, fen1, fbuf1, rbuf1, sbuf1, ebuf1, qbs1, qbr1,
@@ -66,11 +66,15 @@
     own0 = HH * core
     other0 = HH * (1 - core)
 
+    def half(ref, h0):
+        return ref.at[:, pl.ds(pl.multiple_of(h0 * HD, HR), HR)]
+
     loads = [
         pltpu.make_async_copy(src, dst, in_sem.at[i])
         for i, (src, dst) in enumerate(
             (
-                (seg_hbm, seg_ref), (small_hbm, small_ref), (k_hbm, kv), (v_hbm, vv),
+                (half(k_hbm, other0), half(kv, other0)), (half(v_hbm, other0), half(vv, other0)),
+                (half(k_hbm, own0), half(kv, own0)), (half(v_hbm, own0), half(vv, own0)),
                 (q_hbm, qv), (g_hbm, gv), (o_hbm, ov),
             )
         )
@@ -121,11 +125,9 @@
 
     iota = lax.broadcasted_iota(jnp.int32, (BLOCK, HD), 0).astype(F32)
     first_row = jnp.where(lax.broadcasted_iota(jnp.int32, (16, HD), 0) == 0, 1.0, 0.0).astype(BF16)
-    loads[0].wait()
     for n in range(N):
         seg = jnp.broadcast_to(seg_ref[0:1, rows(n)].astype(F32), (16, BLOCK)).astype(BF16)
         segc[rows(n), :] = tn(seg, first_row)
-    loads[1].wait()
     for h in range(H):
         wl[h] = jnp.exp(-rate(h) * (BLOCK - 1.0 - iota))
         for i, times in enumerate((1.0, float(BLOCK), float(T), 2.0 * T)):
@@ -182,8 +184,8 @@
                 own = jnp.where(before == last, pb, 0.0) * own + f
         return own
 
-    loads[2].wait()
-    loads[3].wait()
+    loads[0].wait()
+    loads[1].wait()
     for i in range(HH):
         pbs0[i * HD : (i + 1) * HD, :] = device_state(other0 + i)
     top = lax.broadcasted_iota(jnp.int32, (8, HD), 0) == 0
@@ -191,6 +193,8 @@
     pl.semaphore_wait(barrier, greeted)
     pair0 = remote(pbs0, pbr0, 0, mate, zme)
     pair0.start()
+    loads[2].wait()
+    loads[3].wait()
     for i in range(HH):
         hfs[i * HD : (i + 1) * HD, :] = device_state(own0 + i)
     pair0.wait_recv()
@@ -316,11 +320,14 @@
     post0.start()
     for i in range(HH):
         chain(own0 + i, kept[i])
-    lax.fori_loop(0, N, cross_own, 0)
+    for n in range(N):
+        cross_own(n, 0)
     post0.wait_recv()
     for i in range(HH):
         chain(other0 + i, qbr0[i * HD : (i + 1) * HD, :])
-    total = lax.fori_loop(0, N, cross_other, jnp.zeros((16, BLOCK), F32))
+    total = jnp.zeros((16, BLOCK), F32)
+    for n in range(N):
+        total = cross_other(n, total)
     zbuf[zme] = total[0 : 2 * N, :]
 
     for i in heads:
@@ -518,7 +525,6 @@
     VM = pltpu.VMEM
     scratch = (
         [VM((T, W), BF16)] * 5
-        + [VM((2 * H, HD), F32), VM((1, T), jnp.int32)]
         + [
             VM((T, HD), F32),
             VM((H, BLOCK, HD), F32),
@@ -568,7 +574,7 @@
     outs = pl.pallas_call(
         functools.partial(kernel, (R, Z, N, H)),
         out_shape=(big, big, big, big, small),
-        in_specs=[hbm] * 7,
+        in_specs=[hbm] * 5 + [vspec] * 2,
         out_specs=(vspec,) * 5,
         scratch_shapes=scratch,
         compiler_params=pltpu.CompilerParams(

time: 46.5 us -> 45.2 us (0.972)
  Pallas kernels: 44.4 us -> 43.1 us
    pallas_call x1, Pallas kernels: 42.2 us -> 41 us  [body(): pl.pallas_call(functools.partial(kernel, (R, Z, N, H)), out_shape=(big, b...]
where the time goes in v5:
time: 45.2 us; the launch traced here: 45.1 us
  Pallas kernels  43.1 us (95%)
  local copies, waits for them, and re-layouts  1.25 us (3%)
  between operations  0.66 us (1%)
    pallas_call x1, Pallas kernels, body(): pl.pallas_call(functools.partial(kernel, (R, Z, N, H)), out_shape=(big, b...  41 us
    pallas_call x1, Pallas kernels, body(): pl.pallas_call(functools.partial(mover, pieces), out_shape=(big, big, big...  2.15 us
    unnamed x6, local copies, waits for them, and re-layouts  1.18 us

profile of v5, /device:TPU:1, one launch (start us, length us, event | category | flops | bytes accessed | tf_op | source)
XLA Modules:
  0.0 45.1 jit_solution(7196444536538649010)
XLA Ops:
  0.6 0.0 copy-start.2
  0.6 0.0 copy-start.1
  0.7 0.6 %copy-done.2 = f32[4]{0:T(128)S(1)} copy-done((f32[4]{0:T(128)S(1)}, f32[4]{0:T(128)}, u32[]{:S(2)}) %copy-start.2) | copy-done | bytes 40
  1.3 0.0 copy-start
  1.3 0.1 pad.1.clone
  1.4 0.0 copy-done.1
  1.4 0.1 pad_maximum_fusion.small_ref
  1.4 0.5 %copy-done = s32[1024]{0:T(1024)S(1)} copy-done((s32[1024]{0:T(1024)S(1)}, s32[1024]{0:T(1024)}, u32[]{:S(2)}) %copy-start) | copy-done | bytes 4120
  2.0 41.0 %shard_map.119 = (bf16[1024,512]{1,0:T(8,128)(2,1)S(1)}, bf16[1024,512]{1,0:T(8,128)(2,1)S(1)}, bf16[1024,512]{1,0:T(8,128)(2,1)S(1)}, bf16[1024,512]{1,0:T(8,128)(2,1)S(1)}, f32[1,512]{1,0:T(1,128)S(1)}) custom-call(bf16[1024,512]{1,0:T(8,128)(2,1)} %q_hbm.1, bf16[1024,512]{1,0:T(8,128)(2,1)} %k_hbm.1, bf16[1024,512]{1,0:T(8,128)(2,1)} %v_hbm.1, ...), custom_call_target="tpu_custom_call" | custom-call | tf_op jit(solution)/shard_map/pallas_call | solution.py:574
  43.0 2.1 %shard_map.120 = (bf16[1024,512]{1,0:T(8,128)(2,1)}, bf16[1024,512]{1,0:T(8,128)(2,1)}, bf16[1024,512]{1,0:T(8,128)(2,1)}, bf16[1024,512]{1,0:T(8,128)(2,1)}, f32[1,512]{1,0:T(1,128)}) custom-call(bf16[1024,512]{1,0:T(8,128)(2,1)S(1)} %get-tuple-element.15.refs_0_, bf16[1024,512]{1,0:T(8,128)(2,1)S(1)} %get-tuple-element.16.refs_1_, ...), custom_call_target="tpu_custom_call" | custom-call | tf_op jit(solution)/shard_map/pallas_call | solution.py:588
Async XLA Ops:
  0.6 0.7 %copy-start.2 = (f32[4]{0:T(128)S(1)}, f32[4]{0:T(128)}, u32[]{:S(2)}) copy-start(f32[4]{0:T(128)} %param.14) | copy-start | bytes 52
  0.6 0.7 %copy-start.1 = (f32[512]{0:T(512)S(1)}, f32[512]{0:T(512)}, u32[]{:S(2)}) copy-start(f32[512]{0:T(512)} %param.13) | copy-start | bytes 6148
  1.3 0.7 %copy-start = (s32[1024]{0:T(1024)S(1)}, s32[1024]{0:T(1024)}, u32[]{:S(2)}) copy-start(s32[1024]{0:T(1024)} %param.15) | copy-start | bytes 12292

commit v6 on v5

--- a/solution.py
+++ b/solution.py
@@ -584,7 +584,7 @@
         queries, keys, values, gate, grad_out,
         small_in, segment_ids.reshape(1, T),
     )
-    pieces = (4, 4, 4, 4, 1)
+    pieces = (1, 1, 1, 1, 1)
     moved = pl.pallas_call(
         functools.partial(mover, pieces),
         out_shape=(big, big, big, big, small),

time: 45.2 us -> 45.1 us (level)
  no operation moved by 1% of the time
where the time goes in v6:
time: 45.1 us; the launch traced here: 45 us
  Pallas kernels  43 us (95%)
  local copies, waits for them, and re-layouts  1.25 us (3%)
  between operations  0.66 us (1%)
    pallas_call x1, Pallas kernels, body(): pl.pallas_call(functools.partial(kernel, (R, Z, N, H)), out_shape=(big, b...  41 us
    pallas_call x1, Pallas kernels, body(): pl.pallas_call(functools.partial(mover, pieces), out_shape=(big, big, big...  2.05 us
    unnamed x6, local copies, waits for them, and re-layouts  1.18 us

profile of v6, /device:TPU:1, one launch (start us, length us, event | category | flops | bytes accessed | tf_op | source)
XLA Modules:
  0.0 45.0 jit_solution(12181203109822555749)
XLA Ops:
  0.6 0.0 copy-start.2
  0.6 0.0 copy-start.1
  0.7 0.6 %copy-done.2 = f32[4]{0:T(128)S(1)} copy-done((f32[4]{0:T(128)S(1)}, f32[4]{0:T(128)}, u32[]{:S(2)}) %copy-start.2) | copy-done | bytes 40
  1.3 0.0 copy-start
  1.3 0.1 pad.1.clone
  1.4 0.0 copy-done.1
  1.4 0.1 pad_maximum_fusion.small_ref
  1.4 0.5 %copy-done = s32[1024]{0:T(1024)S(1)} copy-done((s32[1024]{0:T(1024)S(1)}, s32[1024]{0:T(1024)}, u32[]{:S(2)}) %copy-start) | copy-done | bytes 4120
  2.0 41.0 %shard_map.119 = (bf16[1024,512]{1,0:T(8,128)(2,1)S(1)}, bf16[1024,512]{1,0:T(8,128)(2,1)S(1)}, bf16[1024,512]{1,0:T(8,128)(2,1)S(1)}, bf16[1024,512]{1,0:T(8,128)(2,1)S(1)}, f32[1,512]{1,0:T(1,128)S(1)}) custom-call(bf16[1024,512]{1,0:T(8,128)(2,1)} %q_hbm.1, bf16[1024,512]{1,0:T(8,128)(2,1)} %k_hbm.1, bf16[1024,512]{1,0:T(8,128)(2,1)} %v_hbm.1, ...), custom_call_target="tpu_custom_call" | custom-call | tf_op jit(solution)/shard_map/pallas_call | solution.py:574
  43.0 2.1 %shard_map.120 = (bf16[1024,512]{1,0:T(8,128)(2,1)}, bf16[1024,512]{1,0:T(8,128)(2,1)}, bf16[1024,512]{1,0:T(8,128)(2,1)}, bf16[1024,512]{1,0:T(8,128)(2,1)}, f32[1,512]{1,0:T(1,128)}) custom-call(bf16[1024,512]{1,0:T(8,128)(2,1)S(1)} %get-tuple-element.15.refs_0_, bf16[1024,512]{1,0:T(8,128)(2,1)S(1)} %get-tuple-element.16.refs_1_, ...), custom_call_target="tpu_custom_call" | custom-call | tf_op jit(solution)/shard_map/pallas_call | solution.py:588
Async XLA Ops:
  0.6 0.7 %copy-start.2 = (f32[4]{0:T(128)S(1)}, f32[4]{0:T(128)}, u32[]{:S(2)}) copy-start(f32[4]{0:T(128)} %param.14) | copy-start | bytes 52
  0.6 0.7 %copy-start.1 = (f32[512]{0:T(512)S(1)}, f32[512]{0:T(512)}, u32[]{:S(2)}) copy-start(f32[512]{0:T(512)} %param.13) | copy-start | bytes 6148
  1.3 0.7 %copy-start = (s32[1024]{0:T(1024)S(1)}, s32[1024]{0:T(1024)}, u32[]{:S(2)}) copy-start(s32[1024]{0:T(1024)} %param.15) | copy-start | bytes 12292
